TPU v7x, 128 devices: a whole 4x4x4 slice. The times are simulated.
128 devices in a mesh: dp: 32 (over x_lo, z, y), section: 4 (over x_hi, core).
Axes of the slice: x: 4 (x_hi: 2, x_lo: 2; x = x_hi * 2 + x_lo), y: 4, z: 4, core: 2. Of those that a mesh axis runs over, the one named last changes fastest.
Arguments:
- canvas_in: bfloat16 [64, 400, 1152], P('dp', None, 'section'), may hold values from -6 to 6
- conditioning: bfloat16 [64, 1152], P('dp'), may hold values from -6 to 6
- grid_shape: int32 [64], P('dp'), may hold values from 0 to 2, as said below
- kept_rank: int32 [64, 128], P('dp'), may hold values from 0 to 255, as said below
- first_weight: bfloat16 [4, 1152, 4608], P('section')
- second_weight: bfloat16 [4, 4608, 1152], P('section')
- modulation_weight: bfloat16 [4, 1152, 3456], P('section')
- modulation_bias: float32 [4, 3456], P('section'), may hold values from -3 to 3
- out_grad: bfloat16 [64, 400, 1152], P('dp', None, 'section'), may hold values from -6 to 6
Outputs:
- result: bfloat16 [64, 400, 1152], P('dp', None, 'section')
- canvas_grad: bfloat16 [64, 400, 1152], P('dp', None, 'section')
- first_grad: float32 [4, 1152, 4608], P('section', None, 'dp')
- second_grad: float32 [4, 4608, 1152], P('section', 'dp')
- modulation_grad: float32 [4, 1152, 3456], P('section')
- bias_grad: float32 [4, 3456], P('section')
Inputs may be any that keep to these rules, and one draw needn't show every extreme that they name: `grid_shape`: 0, 1 or 2 for each canvas. `kept_rank`: each row holds 128 different token numbers in increasing order, all below the number of real tokens of its canvas.
All inputs are finite; a program needn't handle non-finite values.
Results may differ from a plain program's by a relative error of at most 0.025.
Values may be sent and summed in bfloat16 or wider, within the bound.
A program may use at most 384 MiB of HBM per device.

v0:
```python
import math

import jax
import jax.numpy as jnp
from jax import lax
from jax.sharding import PartitionSpec as P

HEADS = 16
SIDE = 20
VALID = 256


EPSILON = 1e-06
HIGHEST_PRECISION = lax.Precision.HIGHEST
CONTRACT_ROWS = (((0,), (0,)), ((), ()))
CONTRACT_COLUMNS = (((1,), (1,)), ((), ()))


def shortened(value):
    return jax.tree.map(lambda a: a.astype(jnp.bfloat16) if a.dtype == jnp.float32 else a, value)


def shifted(value, axis, by):
    length = lax.axis_size(axis)
    pairs = [(i, i + by) for i in range(length) if 0 <= i + by < length]
    return lax.ppermute(value, axis, pairs)


def broadcast(value, axis, source):
    kept = jnp.where(lax.axis_index(axis) == source, value, 0).astype(value.dtype)
    return lax.psum(kept, axis)


def gelu_tanh(values):
    return jax.nn.gelu(values, approximate=True)


def modulate(rows_float, norm_shift, norm_scale):
    mean_row = jnp.mean(rows_float, axis=-1, keepdims=True)
    centred = rows_float - mean_row
    variance = jnp.mean(centred * centred, axis=-1, keepdims=True)
    return centred * lax.rsqrt(variance + EPSILON) * (1.0 + norm_scale) + norm_shift


def canvas_layout(shape_id):
    grid_rows = jnp.where(shape_id == 1, 12, jnp.where(shape_id == 2, 20, 16)).astype(jnp.int32)
    grid_width = jnp.where(shape_id == 1, 20, jnp.where(shape_id == 2, 12, 16)).astype(jnp.int32)
    token_order = jnp.arange(VALID, dtype=jnp.int32)
    token_live = token_order < grid_rows * grid_width
    token_slot = jnp.where(
        token_live, token_order // grid_width * SIDE + token_order % grid_width, 0
    )
    slot_index = jnp.arange(SIDE * SIDE, dtype=jnp.int32)
    slot_line = slot_index // SIDE
    slot_column = slot_index % SIDE
    filled = (slot_line < grid_rows) & (slot_column < grid_width)
    slot_token = jnp.where(filled, slot_line * grid_width + slot_column, 0)
    return (token_slot, token_live, slot_token, filled)


def pick_rows(table, picks):
    return jnp.take(table, picks, axis=0)


def attention_parts(rows_low, weights, modulation, key_mask):
    model_width = rows_low.shape[1]
    row_count = rows_low.shape[0]
    head_size = model_width // HEADS
    factor = 1.0 / math.sqrt(head_size)
    rows_float = rows_low.astype(jnp.float32)
    hidden_float, pull_norm = jax.vjp(
        modulate, rows_float, modulation[:model_width], modulation[model_width : 2 * model_width]
    )
    hidden = hidden_float.astype(jnp.bfloat16)
    projected = jnp.dot(
        hidden, weights[:, : 3 * model_width], preferred_element_type=jnp.float32
    ).astype(jnp.bfloat16)
    heads_split = projected.reshape(row_count, 3, HEADS, head_size)
    scores = (
        jnp.einsum(
            "qhd,khd->hqk", heads_split[:, 0], heads_split[:, 1], preferred_element_type=jnp.float32
        )
        * factor
    )
    scores = jnp.where(key_mask[None, None, :], scores, -1000000000.0)
    softmaxed = jax.nn.softmax(scores, axis=-1)
    soft_low = softmaxed.astype(jnp.bfloat16)
    mixed_rows = jnp.einsum(
        "hqk,khd->qhd", soft_low, heads_split[:, 2], preferred_element_type=jnp.float32
    )
    mixed_rows = mixed_rows.reshape(row_count, model_width).astype(jnp.bfloat16)
    branch = jnp.dot(mixed_rows, weights[:, 3 * model_width :], preferred_element_type=jnp.float32)
    out_rows = rows_float + modulation[2 * model_width :] * branch
    return (
        out_rows,
        (hidden, heads_split, softmaxed, soft_low, mixed_rows, branch, pull_norm, factor),
    )


def attention_backward(rows_low, weights, modulation, key_mask, upstream):
    model_width = rows_low.shape[1]
    row_count = rows_low.shape[0]
    head_size = model_width // HEADS
    _, kept_parts = attention_parts(rows_low, weights, modulation, key_mask)
    hidden, heads_split, softmaxed, soft_low, mixed_rows, branch, pull_norm, factor = kept_parts
    gate_grad = jnp.sum(upstream * branch, axis=0)
    branch_grad = (upstream * modulation[2 * model_width :]).astype(jnp.bfloat16)
    out_part = lax.dot_general(
        mixed_rows, branch_grad, CONTRACT_ROWS, preferred_element_type=jnp.float32
    )
    mixed_grad = lax.dot_general(
        branch_grad,
        weights[:, 3 * model_width :],
        CONTRACT_COLUMNS,
        preferred_element_type=jnp.float32,
    )
    mixed_grad = mixed_grad.astype(jnp.bfloat16).reshape(row_count, HEADS, head_size)
    soft_grad = jnp.einsum(
        "qhd,khd->hqk", mixed_grad, heads_split[:, 2], preferred_element_type=jnp.float32
    )
    value_grad = jnp.einsum(
        "hqk,qhd->khd", soft_low, mixed_grad, preferred_element_type=jnp.float32
    )
    score_grad = softmaxed * (soft_grad - jnp.sum(softmaxed * soft_grad, axis=-1, keepdims=True))
    score_grad = score_grad.astype(jnp.bfloat16)
    query_grad = (
        jnp.einsum(
            "hqk,khd->qhd", score_grad, heads_split[:, 1], preferred_element_type=jnp.float32
        )
        * factor
    )
    key_grad = (
        jnp.einsum(
            "hqk,qhd->khd", score_grad, heads_split[:, 0], preferred_element_type=jnp.float32
        )
        * factor
    )
    joined = (
        jnp.stack([query_grad, key_grad, value_grad], axis=1)
        .reshape(row_count, 3 * model_width)
        .astype(jnp.bfloat16)
    )
    in_part = lax.dot_general(hidden, joined, CONTRACT_ROWS, preferred_element_type=jnp.float32)
    hidden_grad = lax.dot_general(
        joined, weights[:, : 3 * model_width], CONTRACT_COLUMNS, preferred_element_type=jnp.float32
    )
    rows_grad, shift_grad, scale_grad = pull_norm(hidden_grad)
    weight_part = jnp.concatenate([in_part, out_part], axis=1)
    return (upstream + rows_grad, weight_part, jnp.concatenate([shift_grad, scale_grad, gate_grad]))


def feed_parts(rows_low, first_matrix, second_matrix, modulation):
    model_width = rows_low.shape[1]
    rows_float = rows_low.astype(jnp.float32)
    hidden_float, pull_norm = jax.vjp(
        modulate, rows_float, modulation[:model_width], modulation[model_width : 2 * model_width]
    )
    hidden = hidden_float.astype(jnp.bfloat16)
    inner = jnp.dot(hidden, first_matrix, preferred_element_type=jnp.float32)
    active_float, pull_gelu = jax.vjp(gelu_tanh, inner)
    active = active_float.astype(jnp.bfloat16)
    branch = jnp.dot(active, second_matrix, preferred_element_type=jnp.float32)
    out_rows = rows_float + modulation[2 * model_width :] * branch
    return (out_rows, (hidden, active, branch, pull_norm, pull_gelu))


def feed_backward(rows_low, first_matrix, second_matrix, modulation, upstream):
    model_width = rows_low.shape[1]
    _, kept_parts = feed_parts(rows_low, first_matrix, second_matrix, modulation)
    hidden, active, branch, pull_norm, pull_gelu = kept_parts
    gate_grad = jnp.sum(upstream * branch, axis=0)
    branch_grad = (upstream * modulation[2 * model_width :]).astype(jnp.bfloat16)
    second_part = lax.dot_general(
        active, branch_grad, CONTRACT_ROWS, preferred_element_type=jnp.float32
    )
    active_grad = lax.dot_general(
        branch_grad, second_matrix, CONTRACT_COLUMNS, preferred_element_type=jnp.float32
    )
    inner_grad = pull_gelu(active_grad)[0].astype(jnp.bfloat16)
    first_part = lax.dot_general(
        hidden, inner_grad, CONTRACT_ROWS, preferred_element_type=jnp.float32
    )
    hidden_grad = lax.dot_general(
        inner_grad, first_matrix, CONTRACT_COLUMNS, preferred_element_type=jnp.float32
    )
    rows_grad, shift_grad, scale_grad = pull_norm(hidden_grad)
    return (
        upstream + rows_grad,
        first_part,
        second_part,
        jnp.concatenate([shift_grad, scale_grad, gate_grad]),
    )


def local(
    canvas_in,
    conditioning,
    grid_shape,
    kept_rank,
    first_weight,
    second_weight,
    modulation_weight,
    modulation_bias,
    out_grad,
):
    section_index = lax.axis_index("section")
    sections = lax.axis_size("section")
    micro_count = canvas_in.shape[0]
    first_local = first_weight[0]
    second_local = second_weight[0]
    model_width = first_local.shape[0]
    hidden_width = first_local.shape[1]
    token_slot, token_live, slot_token, filled = jax.vmap(canvas_layout)(grid_shape)
    signal = jax.nn.silu(conditioning.astype(jnp.float32)).astype(jnp.bfloat16)
    modulation = (
        jnp.dot(signal, modulation_weight[0], preferred_element_type=jnp.float32)
        + modulation_bias[0]
    )
    whole_in, whole_grad = (
        lax.all_gather(canvas_in, "section", axis=2, tiled=True),
        lax.all_gather(out_grad, "section", axis=2, tiled=True),
    )
    zero_low = jnp.zeros((), jnp.bfloat16)
    packed_in = jnp.where(
        token_live[:, :, None], jax.vmap(pick_rows)(whole_in, token_slot), zero_low
    )
    packed_grad = jnp.where(
        token_live[:, :, None], jax.vmap(pick_rows)(whole_grad, token_slot), zero_low
    )
    every_key = jnp.ones((kept_rank.shape[1],), dtype=bool)

    def section_attention(rows_low, micro_index):
        out_rows, _ = attention_parts(
            rows_low, first_local, modulation[micro_index], token_live[micro_index]
        )
        return out_rows.astype(jnp.bfloat16)

    def section_feed(rows_low, micro_index):
        out_rows, _ = feed_parts(rows_low, first_local, second_local, modulation[micro_index])
        return out_rows.astype(jnp.bfloat16)

    def section_routed_attention(rows_low, micro_index):
        picks = kept_rank[micro_index]
        out_rows, _ = attention_parts(
            pick_rows(rows_low, picks), first_local, modulation[micro_index], every_key
        )
        return rows_low.at[picks].set(out_rows.astype(jnp.bfloat16))

    def section_routed_feed(rows_low, micro_index):
        picks = kept_rank[micro_index]
        out_rows, _ = feed_parts(
            pick_rows(rows_low, picks), first_local, second_local, modulation[micro_index]
        )
        return rows_low.at[picks].set(out_rows.astype(jnp.bfloat16))

    def section_waiting(rows_low, micro_index):
        return rows_low

    forward_sections = [
        section_attention,
        section_feed,
        section_routed_attention,
        section_routed_feed,
        section_waiting,
    ]

    def forward_tick(carry, tick_index):
        incoming, stash_rows, final_rows = carry
        micro = tick_index - section_index
        active = (micro >= 0) & (micro < micro_count)
        micro_index = jnp.clip(micro, 0, micro_count - 1)
        source = jnp.where(section_index == 0, packed_in[micro_index], incoming)
        chosen_section = jnp.where(active, section_index, 4)
        produced = lax.switch(chosen_section, forward_sections, source, micro_index)
        stash_rows = stash_rows.at[micro_index].set(
            jnp.where(active, source, stash_rows[micro_index])
        )
        at_last = active & (section_index == sections - 1)
        final_rows = final_rows.at[micro_index].set(
            jnp.where(at_last, produced, final_rows[micro_index])
        )
        incoming = jax.tree.map(
            lambda part, own: part.astype(own.dtype),
            shifted(shortened(produced), "section", 1),
            produced,
        )
        return ((incoming, stash_rows, final_rows), None)

    rows_shape = (micro_count, VALID, model_width)
    start_rows = jnp.zeros((VALID, model_width), jnp.bfloat16)
    start_stash = jnp.zeros(rows_shape, jnp.bfloat16)
    (_, stash_rows, final_rows), _ = lax.scan(
        forward_tick, (start_rows, start_stash, start_stash), jnp.arange(micro_count + sections - 1)
    )
    result_canvas = jnp.where(
        filled[:, :, None], jax.vmap(pick_rows)(final_rows, slot_token), zero_low
    )
    result_full = broadcast(result_canvas, "section", sections - 1)

    def back_attention(rows_low, upstream, micro_index):
        rows_grad, weight_part, modulation_part = attention_backward(
            rows_low, first_local, modulation[micro_index], token_live[micro_index], upstream
        )
        return (
            rows_grad,
            weight_part,
            jnp.zeros((hidden_width, model_width), jnp.float32),
            modulation_part,
        )

    def back_feed(rows_low, upstream, micro_index):
        return feed_backward(rows_low, first_local, second_local, modulation[micro_index], upstream)

    def back_routed_attention(rows_low, upstream, micro_index):
        picks = kept_rank[micro_index]
        rows_grad, weight_part, modulation_part = attention_backward(
            pick_rows(rows_low, picks),
            first_local,
            modulation[micro_index],
            every_key,
            pick_rows(upstream, picks),
        )
        return (
            upstream.at[picks].set(rows_grad),
            weight_part,
            jnp.zeros((hidden_width, model_width), jnp.float32),
            modulation_part,
        )

    def back_routed_feed(rows_low, upstream, micro_index):
        picks = kept_rank[micro_index]
        rows_grad, first_part, second_part, modulation_part = feed_backward(
            pick_rows(rows_low, picks),
            first_local,
            second_local,
            modulation[micro_index],
            pick_rows(upstream, picks),
        )
        return (upstream.at[picks].set(rows_grad), first_part, second_part, modulation_part)

    def back_waiting(rows_low, upstream, micro_index):
        return (
            jnp.zeros((VALID, model_width), jnp.float32),
            jnp.zeros((model_width, hidden_width), jnp.float32),
            jnp.zeros((hidden_width, model_width), jnp.float32),
            jnp.zeros((3 * model_width,), jnp.float32),
        )

    backward_sections = [
        back_attention,
        back_feed,
        back_routed_attention,
        back_routed_feed,
        back_waiting,
    ]

    def backward_tick(carry, tick_index):
        incoming, first_total, second_total, modulation_grads, input_rows = carry
        micro = tick_index - (sections - 1 - section_index)
        active = (micro >= 0) & (micro < micro_count)
        micro_index = jnp.clip(micro, 0, micro_count - 1)
        upstream = jnp.where(
            section_index == sections - 1, packed_grad[micro_index], incoming
        ).astype(jnp.float32)
        chosen_section = jnp.where(active, section_index, 4)
        sent_rows, first_part, second_part, modulation_part = lax.switch(
            chosen_section, backward_sections, stash_rows[micro_index], upstream, micro_index
        )
        first_total = first_total + first_part
        second_total = second_total + second_part
        modulation_grads = modulation_grads.at[micro_index].add(modulation_part)
        sent_low = sent_rows.astype(jnp.bfloat16)
        at_first = active & (section_index == 0)
        input_rows = input_rows.at[micro_index].set(
            jnp.where(at_first, sent_low, input_rows[micro_index])
        )
        incoming = shifted(sent_low, "section", -1)
        return ((incoming, first_total, second_total, modulation_grads, input_rows), None)

    start_back = (
        start_rows,
        jnp.zeros((model_width, hidden_width), jnp.float32),
        jnp.zeros((hidden_width, model_width), jnp.float32),
        jnp.zeros((micro_count, 3 * model_width), jnp.float32),
        start_stash,
    )
    (_, first_total, second_total, modulation_grads, input_rows), _ = lax.scan(
        backward_tick, start_back, jnp.arange(micro_count + sections - 1)
    )
    grad_canvas = jnp.where(
        filled[:, :, None], jax.vmap(pick_rows)(input_rows, slot_token), zero_low
    )
    grad_full = broadcast(grad_canvas, "section", 0)
    quarter = model_width // sections
    result_part = lax.dynamic_slice_in_dim(result_full, section_index * quarter, quarter, axis=2)
    grad_part = lax.dynamic_slice_in_dim(grad_full, section_index * quarter, quarter, axis=2)
    first_sum = lax.psum_scatter(
        first_total.astype(jnp.bfloat16), "dp", scatter_dimension=1, tiled=True
    ).astype(jnp.float32)
    second_sum = lax.psum_scatter(
        second_total.astype(jnp.bfloat16), "dp", scatter_dimension=0, tiled=True
    ).astype(jnp.float32)
    signal_float = signal.astype(jnp.float32)
    local_product = lax.dot_general(
        signal_float,
        modulation_grads,
        CONTRACT_ROWS,
        precision=HIGHEST_PRECISION,
        preferred_element_type=jnp.float32,
    )
    weight_sum, bias_sum = (
        lax.psum(local_product.astype(jnp.bfloat16), "dp").astype(jnp.float32),
        lax.psum(jnp.sum(modulation_grads, axis=0).astype(jnp.bfloat16), "dp").astype(jnp.float32),
    )
    return (
        result_part,
        grad_part,
        first_sum[None],
        second_sum[None],
        weight_sum[None],
        bias_sum[None],
    )


def solution(mesh):
    placed = (
        P("dp", None, "section"),
        P("dp", None),
        P("dp"),
        P("dp", None),
        P("section", None, None),
        P("section", None, None),
        P("section", None, None),
        P("section", None),
        P("dp", None, "section"),
    )
    return jax.shard_map(
        local,
        mesh=mesh,
        in_specs=placed,
        out_specs=(
            P("dp", None, "section"),
            P("dp", None, "section"),
            P("section", None, "dp"),
            P("section", "dp", None),
            P("section", None, None),
            P("section", None),
        ),
        check_vma=False,
    )
```

profile of v0, /device:TPU:2, one launch (start us, length us, event | category | flops | bytes accessed | tf_op | source)
XLA Modules:
  0.0 1702.3 jit_solution(16565363587030842404)
XLA Ops:
  19.4 20.4 %all-gather.3.cloned.1.call-done = bf16[2,400,1152]{1,0,2:T(2,128)(2,1)} async-done(((bf16[2,400,288]{1,0,2:T(2,128)(2,1)}), bf16[2,400,1152]{1,0,2:T(2,128)(2,1)}) %all-gather.3.cloned.1.call-update) | async-done | bytes 1843216 | tf_op jit(solution)/shard_map/all_gather | solution.py:220
  51.3 18.4 %all-gather.5.cloned.1.call-done = bf16[2,400,1152]{1,0,2:T(2,128)(2,1)} async-done(((bf16[2,400,288]{1,0,2:T(2,128)(2,1)}), bf16[2,400,1152]{1,0,2:T(2,128)(2,1)}) %all-gather.5.cloned.1.call-update) | async-done | bytes 1843216 | tf_op jit(solution)/shard_map/all_gather | solution.py:221
  75.4 8.4 gather_fusion.8
  88.0 144.2 %while.40 = (s32[]{:T(128)}, bf16[256,1152]{1,0:T(8,128)(2,1)}, bf16[2,256,1152]{2,1,0:T(8,128)(2,1)S(1)}, bf16[2,256,1152]{2,1,0:T(8,128)(2,1)S(1)}, s32[5]{0:T...) while((s32[]{:T(128)}, bf16[256,1152]{1,0:T(8,128)(2,1)}, ...), condition=%wide.region_21.24_spmd.clone, body=%wide.region_0.23_spmd.clone.sunk | while | flops 5452629504 | bytes 59922492 | solution.py:292
  93.4 19.1 %conditional.6 = (bf16[256,1152]{1,0:T(8,128)(2,1)}) conditional(s32[]{:T(128)} %clamp.46, (bf16[256,1152]{1,0:T(8,128)(2,1)S(1)}, s32[]{:T(128)}, f32[2,3456]{1,0:T(2,128)}, bf16[1152,4608]{1,0:T(8,128)(2,1)}, s32[2,256]{1,0:T(2,128)S(1)}, /*index=5*/s32[2]{0:T(128)}) %tuple.182, (bf16[256,1152]{1,0:T(8,128)(2,1)S(1)}, ...), branch_computations={%region_1.6_spmd, %region_6.9_spmd, %region_9.16_spmd, %region_15.... | conditional | flops 5451154944 | bytes 38685856 | solution.py:274
  121.6 19.1 %conditional.6 = (bf16[256,1152]{1,0:T(8,128)(2,1)}) conditional(s32[]{:T(128)} %clamp.46, (bf16[256,1152]{1,0:T(8,128)(2,1)S(1)}, s32[]{:T(128)}, f32[2,3456]{1,0:T(2,128)}, bf16[1152,4608]{1,0:T(8,128)(2,1)}, s32[2,256]{1,0:T(2,128)S(1)}, /*index=5*/s32[2]{0:T(128)}) %tuple.182, (bf16[256,1152]{1,0:T(8,128)(2,1)S(1)}, ...), branch_computations={%region_1.6_spmd, %region_6.9_spmd, %region_9.16_spmd, %region_15.... | conditional | flops 5451154944 | bytes 38685856 | solution.py:274
  122.9 7.2 fusion.7
  150.7 20.1 %collective-permute-start = (bf16[256,1152]{1,0:T(8,128)(2,1)}, bf16[256,1152]{1,0:T(8,128)(2,1)S(1)}, u32[]{:S(2)}, u32[]{:S(2)}) collective-permute-start(bf16[256,1152]{1,0:T(8,128)(2,1)} %get-tuple-element.1096), channel_id=1, source_target_pairs={{0,1},{1,2},{2,3},{4,5},{5,6},{6,7},{8,9},{9,10},{10,11},{12,13},{... | collective-permute-start | bytes 1769480 | tf_op jit(solution)/shard_map/while/body/eval_jaxpr/ppermute | solution.py:26
  179.4 13.4 collective-permute-start
  201.3 28.3 %collective-permute-start = (bf16[256,1152]{1,0:T(8,128)(2,1)}, bf16[256,1152]{1,0:T(8,128)(2,1)S(1)}, u32[]{:S(2)}, u32[]{:S(2)}) collective-permute-start(bf16[256,1152]{1,0:T(8,128)(2,1)} %get-tuple-element.1096), channel_id=1, source_target_pairs={{0,1},{1,2},{2,3},{4,5},{5,6},{6,7},{8,9},{9,10},{10,11},{12,13},{... | collective-permute-start | bytes 1769480 | tf_op jit(solution)/shard_map/while/body/eval_jaxpr/ppermute | solution.py:26
  235.0 570.9 %while.41 = (s32[]{:T(128)}, bf16[256,1152]{1,0:T(8,128)(2,1)}, f32[1152,4608]{1,0:T(8,128)}, f32[4608,1152]{1,0:T(8,128)}, f32[2,3456]{1,0:T(2,128)}, /*index=5...) while((s32[]{:T(128)}, bf16[256,1152]{1,0:T(8,128)(2,1)}, ...), condition=%wide.region_67.72_spmd.clone, body=%wide.region_23.71_spmd.clone.sunk | while | flops 16389749760 | bytes 453526592 | solution.py:387
  239.3 48.5 %conditional.7 = (f32[1152,4608]{1,0:T(8,128)}, f32[4608,1152]{1,0:T(8,128)}, bf16[256,1152]{1,0:T(8,128)(2,1)}, f32[1,3456]{1,0:T(1,128)S(1)}) conditional(s32[]{:T(128)} %clamp.47, (bf16[256,1152]{1,0:T(8,128)(2,1)S(1)}, s32[]{:T(128)}, f32[2,3456]{1,0:T(2,128)S(1)}, bf16[1152,4608]{1,0:T(8,128)(2,1)}, ...), branch_computations={%region_24.37_spmd, %region_35.45_spmd, %region_43.58_spmd, %regio... | conditional | flops 16367329280 | bytes 243947808 | solution.py:366
  268.3 9.8 broadcast.681
  278.1 8.6 broadcast.682
  293.4 18.5 %select_add_fusion.4 = f32[1152,4608]{1,0:T(8,128)} fusion(f32[1152,4608]{1,0:T(8,128)} %get-tuple-element.936, f32[1152,4608]{1,0:T(8,128)} %get-tuple-element.1046, pred[]{:T(512)S(6)} %compare.65), kind=kLoop, calls=%fused_computation.445.clone.1 | loop fusion | flops 10616832 | bytes 63700992 | tf_op jit(solution)/shard_map/while/body/eval_jaxpr/add | solution.py:369
  313.9 7.9 select_add_fusion.5
  328.6 48.8 %conditional.7 = (f32[1152,4608]{1,0:T(8,128)}, f32[4608,1152]{1,0:T(8,128)}, bf16[256,1152]{1,0:T(8,128)(2,1)}, f32[1,3456]{1,0:T(1,128)S(1)}) conditional(s32[]{:T(128)} %clamp.47, (bf16[256,1152]{1,0:T(8,128)(2,1)S(1)}, s32[]{:T(128)}, f32[2,3456]{1,0:T(2,128)S(1)}, bf16[1152,4608]{1,0:T(8,128)(2,1)}, ...), branch_computations={%region_24.37_spmd, %region_35.45_spmd, %region_43.58_spmd, %regio... | conditional | flops 16367329280 | bytes 243947808 | solution.py:366
  357.8 9.8 broadcast.681
  367.6 8.6 broadcast.682
  383.0 22.5 %select_add_fusion.4 = f32[1152,4608]{1,0:T(8,128)} fusion(f32[1152,4608]{1,0:T(8,128)} %get-tuple-element.936, f32[1152,4608]{1,0:T(8,128)} %get-tuple-element.1046, pred[]{:T(512)S(6)} %compare.65), kind=kLoop, calls=%fused_computation.445.clone.1 | loop fusion | flops 10616832 | bytes 63700992 | tf_op jit(solution)/shard_map/while/body/eval_jaxpr/add | solution.py:369
  409.8 16.5 select_add_fusion.5
  433.4 48.5 %conditional.7 = (f32[1152,4608]{1,0:T(8,128)}, f32[4608,1152]{1,0:T(8,128)}, bf16[256,1152]{1,0:T(8,128)(2,1)}, f32[1,3456]{1,0:T(1,128)S(1)}) conditional(s32[]{:T(128)} %clamp.47, (bf16[256,1152]{1,0:T(8,128)(2,1)S(1)}, s32[]{:T(128)}, f32[2,3456]{1,0:T(2,128)S(1)}, bf16[1152,4608]{1,0:T(8,128)(2,1)}, ...), branch_computations={%region_24.37_spmd, %region_35.45_spmd, %region_43.58_spmd, %regio... | conditional | flops 16367329280 | bytes 243947808 | solution.py:366
  462.4 9.8 broadcast.681
  472.2 8.6 broadcast.682
  487.5 22.5 %select_add_fusion.4 = f32[1152,4608]{1,0:T(8,128)} fusion(f32[1152,4608]{1,0:T(8,128)} %get-tuple-element.936, f32[1152,4608]{1,0:T(8,128)} %get-tuple-element.1046, pred[]{:T(512)S(6)} %compare.65), kind=kLoop, calls=%fused_computation.445.clone.1 | loop fusion | flops 10616832 | bytes 63700992 | tf_op jit(solution)/shard_map/while/body/eval_jaxpr/add | solution.py:369
  514.4 16.5 select_add_fusion.5
  537.6 74.9 %conditional.7 = (f32[1152,4608]{1,0:T(8,128)}, f32[4608,1152]{1,0:T(8,128)}, bf16[256,1152]{1,0:T(8,128)(2,1)}, f32[1,3456]{1,0:T(1,128)S(1)}) conditional(s32[]{:T(128)} %clamp.47, (bf16[256,1152]{1,0:T(8,128)(2,1)S(1)}, s32[]{:T(128)}, f32[2,3456]{1,0:T(2,128)S(1)}, bf16[1152,4608]{1,0:T(8,128)(2,1)}, ...), branch_computations={%region_24.37_spmd, %region_35.45_spmd, %region_43.58_spmd, %regio... | conditional | flops 16367329280 | bytes 243947808 | solution.py:366
  538.2 7.2 fusion.81
  582.9 7.7 pad_maximum_fusion
  590.6 8.6 broadcast.650
  618.2 22.5 %select_add_fusion.4 = f32[1152,4608]{1,0:T(8,128)} fusion(f32[1152,4608]{1,0:T(8,128)} %get-tuple-element.936, f32[1152,4608]{1,0:T(8,128)} %get-tuple-element.1046, pred[]{:T(512)S(6)} %compare.65), kind=kLoop, calls=%fused_computation.445.clone.1 | loop fusion | flops 10616832 | bytes 63700992 | tf_op jit(solution)/shard_map/while/body/eval_jaxpr/add | solution.py:369
  645.0 16.5 select_add_fusion.5
  669.6 74.5 %conditional.7 = (f32[1152,4608]{1,0:T(8,128)}, f32[4608,1152]{1,0:T(8,128)}, bf16[256,1152]{1,0:T(8,128)(2,1)}, f32[1,3456]{1,0:T(1,128)S(1)}) conditional(s32[]{:T(128)} %clamp.47, (bf16[256,1152]{1,0:T(8,128)(2,1)S(1)}, s32[]{:T(128)}, f32[2,3456]{1,0:T(2,128)S(1)}, bf16[1152,4608]{1,0:T(8,128)(2,1)}, ...), branch_computations={%region_24.37_spmd, %region_35.45_spmd, %region_43.58_spmd, %regio... | conditional | flops 16367329280 | bytes 243947808 | solution.py:366
  670.2 7.2 fusion.81
  714.3 7.7 pad_maximum_fusion
  722.0 8.6 broadcast.650
  749.7 22.5 %select_add_fusion.4 = f32[1152,4608]{1,0:T(8,128)} fusion(f32[1152,4608]{1,0:T(8,128)} %get-tuple-element.936, f32[1152,4608]{1,0:T(8,128)} %get-tuple-element.1046, pred[]{:T(512)S(6)} %compare.65), kind=kLoop, calls=%fused_computation.445.clone.1 | loop fusion | flops 10616832 | bytes 63700992 | tf_op jit(solution)/shard_map/while/body/eval_jaxpr/add | solution.py:369
  776.6 16.5 select_add_fusion.5
  805.9 19.6 %gather_fusion.9 = bf16[800,1152]{1,0:T(8,128)(2,1)S(1)} fusion(bf16[2,256,1152]{2,1,0:T(8,128)(2,1)} %get-tuple-element.482, s32[800]{0:T(1024)S(1)} %copy-done.6), kind=kCustom, calls=%fused_computation.8.clone | custom fusion | bytes 3692800 | tf_op jit(solution)/shard_map/vmap(jit(_take))/gather | solution.py:62
  828.0 16.7 gather_fusion.7
  854.1 8.6 fusion.316
  862.8 12.2 convert_element_type.219
  875.0 17.5 %copy.95 = bf16[1152,4608]{0,1:T(8,128)(2,1)} copy(f32[1152,4608]{1,0:T(8,128)} %get-tuple-element.483) | data formatting | bytes 31850496 | tf_op jit(solution)/shard_map/while | solution.py:387
  892.6 160.6 %psum.31 = bf16[1,3456]{1,0:T(2,128)(2,1)S(1)} all-reduce(bf16[1,3456]{1,0:T(2,128)(2,1)S(1)} %broadcast_in_dim.293), channel_id=1, replica_groups=mesh['dp'=32,'section'=4] {'dp'}, use_global_device_ids=true, to_apply=%region_73.78 | all-reduce | flops 3456 | bytes 13824 | tf_op jit(solution)/shard_map/psum | solution.py:413
  1057.7 263.6 %all-reduce.4.cloned.1.call-done = bf16[1,1152,3456]{2,1,0:T(8,128)(2,1)} async-done(((bf16[1,1152,3456]{2,1,0:T(8,128)(2,1)}), bf16[1,1152,3456]{2,1,0:T(8,128)(2,1)}) %all-reduce.4.cloned.1.call-update) | async-done | bytes 7962640 | tf_op jit(solution)/shard_map/psum | solution.py:412
  1321.3 10.2 broadcast_in_dim.292
  1331.5 177.0 %reduce-scatter.5.cloned.1.call-done = bf16[144,1152]{1,0:T(8,128)(2,1)} async-done(((bf16[4608,1152]{1,0:T(8,128)(2,1)}), bf16[144,1152]{1,0:T(8,128)(2,1)}) %reduce-scatter.5.cloned.1.call-update) | async-done | bytes 331792 | tf_op jit(solution)/shard_map/reduce_scatter | solution.py:400
  1510.4 182.7 %reduce-scatter.3.cloned.1.call-done = bf16[1152,144]{0,1:T(8,128)(2,1)} async-done(((bf16[1152,4608]{0,1:T(8,128)(2,1)}), bf16[1152,144]{0,1:T(8,128)(2,1)}) %reduce-scatter.3.cloned.1.call-update) | async-done | bytes 331792 | tf_op jit(solution)/shard_map/reduce_scatter | solution.py:397
  (523 shorter events, 285.7 us)
Async XLA Ops:
  7.2 32.7 %all-gather.3.cloned.1.call-start = ((), (), s32[]{:S(2)}) async-start(), calls=%async_computation.2 | async-start | bytes 2949120 | tf_op jit(solution)/shard_map/all_gather | solution.py:220
  9.8 59.9 %all-gather.5.cloned.1.call-start = ((), (), s32[]{:S(2)}) async-start(), calls=%async_computation.3 | async-start | bytes 2949120 | tf_op jit(solution)/shard_map/all_gather | solution.py:221
  12.3 1041.5 %all-reduce.6.cloned.1.call-start = ((), (), s32[]{:S(2)}) async-start(), calls=%async_computation.7 | async-start | bytes 9437184 | tf_op jit(solution)/shard_map/psum | solution.py:31
  112.4 3.2 collective-permute-start
  140.7 3.2 collective-permute-start
  150.7 22.7 %copy-start.19 = (bf16[2,256,1152]{2,1,0:T(8,128)(2,1)S(1)}, bf16[2,256,1152]{2,1,0:T(8,128)(2,1)}, u32[]{:S(2)}) copy-start(bf16[2,256,1152]{2,1,0:T(8,128)(2,1)} %copy-done.18) | copy-start | bytes 3538948 | tf_op jit(solution)/shard_map/while
  150.7 22.7 %copy-start.47 = (s32[3]{0:T(128)S(1)}, s32[3]{0:T(128)}, u32[]{:S(2)}) copy-start(s32[3]{0:T(128)} %get-tuple-element.1149) | copy-start | bytes 40 | tf_op jit(solution)/shard_map/while
  150.7 22.7 %copy-start.63 = (s32[5]{0:T(128)S(1)}, s32[5]{0:T(128)}, u32[]{:S(2)}) copy-start(s32[5]{0:T(128)} %copy-done.62) | copy-start | bytes 64 | tf_op jit(solution)/shard_map/while
  150.7 21.9 %collective-permute-start = (bf16[256,1152]{1,0:T(8,128)(2,1)}, bf16[256,1152]{1,0:T(8,128)(2,1)S(1)}, u32[]{:S(2)}, u32[]{:S(2)}) collective-permute-start(bf16[256,1152]{1,0:T(8,128)(2,1)} %get-tuple-element.1096), channel_id=1, source_target_pairs={{0,1},{1,2},{2,3},{4,5},{5,6},{6,7},{8,9},{9,10},{10,11},{12,13},{... | collective-permute-start | bytes 1769480 | tf_op jit(solution)/shard_map/while/body/eval_jaxpr/ppermute | solution.py:26
  179.4 15.2 collective-permute-start
  201.3 30.9 %copy-start.19 = (bf16[2,256,1152]{2,1,0:T(8,128)(2,1)S(1)}, bf16[2,256,1152]{2,1,0:T(8,128)(2,1)}, u32[]{:S(2)}) copy-start(bf16[2,256,1152]{2,1,0:T(8,128)(2,1)} %copy-done.18) | copy-start | bytes 3538948 | tf_op jit(solution)/shard_map/while
  201.3 30.9 %copy-start.47 = (s32[3]{0:T(128)S(1)}, s32[3]{0:T(128)}, u32[]{:S(2)}) copy-start(s32[3]{0:T(128)} %get-tuple-element.1149) | copy-start | bytes 40 | tf_op jit(solution)/shard_map/while
  201.3 30.9 %copy-start.63 = (s32[5]{0:T(128)S(1)}, s32[5]{0:T(128)}, u32[]{:S(2)}) copy-start(s32[5]{0:T(128)} %copy-done.62) | copy-start | bytes 64 | tf_op jit(solution)/shard_map/while
  201.3 30.0 %collective-permute-start = (bf16[256,1152]{1,0:T(8,128)(2,1)}, bf16[256,1152]{1,0:T(8,128)(2,1)S(1)}, u32[]{:S(2)}, u32[]{:S(2)}) collective-permute-start(bf16[256,1152]{1,0:T(8,128)(2,1)} %get-tuple-element.1096), channel_id=1, source_target_pairs={{0,1},{1,2},{2,3},{4,5},{5,6},{6,7},{8,9},{9,10},{10,11},{12,13},{... | collective-permute-start | bytes 1769480 | tf_op jit(solution)/shard_map/while/body/eval_jaxpr/ppermute | solution.py:26
  235.0 570.9 %copy-start.6 = (s32[800]{0:T(1024)S(1)}, s32[800]{0:T(1024)}, u32[]{:S(2)}) copy-start(s32[800]{0:T(1024)} %reshape.790) | copy-start | bytes 9604
  239.2 49.8 %copy-start = (bf16[2,256,1152]{2,1,0:T(8,128)(2,1)S(1)}, bf16[2,256,1152]{2,1,0:T(8,128)(2,1)}, u32[]{:S(2)}) copy-start(bf16[2,256,1152]{2,1,0:T(8,128)(2,1)} %get-tuple-element.1049) | copy-start | bytes 3538948 | tf_op jit(solution)/shard_map/while
  287.8 35.7 %collective-permute-start.1 = (bf16[256,1152]{1,0:T(8,128)(2,1)}, bf16[256,1152]{1,0:T(8,128)(2,1)}, u32[]{:S(2)}, u32[]{:S(2)}) collective-permute-start(bf16[256,1152]{1,0:T(8,128)(2,1)} %get-tuple-element.935), channel_id=1, source_target_pairs={{1,0},{2,1},{3,2},{5,4},{6,5},{7,6},{9,8},{10,9},{11,10},{13,12},{... | collective-permute-start | bytes 1769480 | tf_op jit(solution)/shard_map/while/body/eval_jaxpr/ppermute | solution.py:26
  328.6 50.1 %copy-start = (bf16[2,256,1152]{2,1,0:T(8,128)(2,1)S(1)}, bf16[2,256,1152]{2,1,0:T(8,128)(2,1)}, u32[]{:S(2)}) copy-start(bf16[2,256,1152]{2,1,0:T(8,128)(2,1)} %get-tuple-element.1049) | copy-start | bytes 3538948 | tf_op jit(solution)/shard_map/while
  377.4 50.6 %collective-permute-start.1 = (bf16[256,1152]{1,0:T(8,128)(2,1)}, bf16[256,1152]{1,0:T(8,128)(2,1)}, u32[]{:S(2)}, u32[]{:S(2)}) collective-permute-start(bf16[256,1152]{1,0:T(8,128)(2,1)} %get-tuple-element.935), channel_id=1, source_target_pairs={{1,0},{2,1},{3,2},{5,4},{6,5},{7,6},{9,8},{10,9},{11,10},{13,12},{... | collective-permute-start | bytes 1769480 | tf_op jit(solution)/shard_map/while/body/eval_jaxpr/ppermute | solution.py:26
  383.0 22.6 %slice-start.1 = ((s8[21233664]{0:T(1024)(128)(4,1)}), s8[4194304]{0:T(1024)(128)(4,1)S(1)}, s32[]{:S(2)}) async-start(s8[21233664]{0:T(1024)(128)(4,1)} %bitcast.268), calls=%async_computation.9 | async-start | bytes 8388608 | tf_op jit(solution)/shard_map/while
  383.0 24.5 %slice-start.2 = ((s8[21233664]{0:T(1024)(128)(4,1)}), s8[4194304]{0:T(1024)(128)(4,1)S(1)}, s32[]{:S(2)}) async-start(s8[21233664]{0:T(1024)(128)(4,1)} %bitcast.268), calls=%async_computation.10 | async-start | bytes 8388608 | tf_op jit(solution)/shard_map/while
  383.0 25.7 %slice-start.3 = ((s8[21233664]{0:T(1024)(128)(4,1)}), s8[4194304]{0:T(1024)(128)(4,1)S(1)}, s32[]{:S(2)}) async-start(s8[21233664]{0:T(1024)(128)(4,1)} %bitcast.268), calls=%async_computation.11 | async-start | bytes 8388608 | tf_op jit(solution)/shard_map/while
  383.0 26.9 %slice-start.4 = ((s8[21233664]{0:T(1024)(128)(4,1)}), s8[4194304]{0:T(1024)(128)(4,1)S(1)}, s32[]{:S(2)}) async-start(s8[21233664]{0:T(1024)(128)(4,1)} %bitcast.268), calls=%async_computation.12 | async-start | bytes 8388608 | tf_op jit(solution)/shard_map/while
  383.0 26.8 %slice-start.5 = ((s8[21233664]{0:T(1024)(128)(4,1)}), s8[262144]{0:T(1024)(128)(4,1)S(1)}, s32[]{:S(2)}) async-start(s8[21233664]{0:T(1024)(128)(4,1)} %bitcast.268), calls=%async_computation.13 | async-start | bytes 524288 | tf_op jit(solution)/shard_map/while
  433.4 49.8 %copy-start = (bf16[2,256,1152]{2,1,0:T(8,128)(2,1)S(1)}, bf16[2,256,1152]{2,1,0:T(8,128)(2,1)}, u32[]{:S(2)}) copy-start(bf16[2,256,1152]{2,1,0:T(8,128)(2,1)} %get-tuple-element.1049) | copy-start | bytes 3538948 | tf_op jit(solution)/shard_map/while
  481.9 50.6 %collective-permute-start.1 = (bf16[256,1152]{1,0:T(8,128)(2,1)}, bf16[256,1152]{1,0:T(8,128)(2,1)}, u32[]{:S(2)}, u32[]{:S(2)}) collective-permute-start(bf16[256,1152]{1,0:T(8,128)(2,1)} %get-tuple-element.935), channel_id=1, source_target_pairs={{1,0},{2,1},{3,2},{5,4},{6,5},{7,6},{9,8},{10,9},{11,10},{13,12},{... | collective-permute-start | bytes 1769480 | tf_op jit(solution)/shard_map/while/body/eval_jaxpr/ppermute | solution.py:26
  487.5 22.6 %slice-start.1 = ((s8[21233664]{0:T(1024)(128)(4,1)}), s8[4194304]{0:T(1024)(128)(4,1)S(1)}, s32[]{:S(2)}) async-start(s8[21233664]{0:T(1024)(128)(4,1)} %bitcast.268), calls=%async_computation.9 | async-start | bytes 8388608 | tf_op jit(solution)/shard_map/while
  487.5 24.5 %slice-start.2 = ((s8[21233664]{0:T(1024)(128)(4,1)}), s8[4194304]{0:T(1024)(128)(4,1)S(1)}, s32[]{:S(2)}) async-start(s8[21233664]{0:T(1024)(128)(4,1)} %bitcast.268), calls=%async_computation.10 | async-start | bytes 8388608 | tf_op jit(solution)/shard_map/while
  487.5 25.7 %slice-start.3 = ((s8[21233664]{0:T(1024)(128)(4,1)}), s8[4194304]{0:T(1024)(128)(4,1)S(1)}, s32[]{:S(2)}) async-start(s8[21233664]{0:T(1024)(128)(4,1)} %bitcast.268), calls=%async_computation.11 | async-start | bytes 8388608 | tf_op jit(solution)/shard_map/while
  487.5 26.9 %slice-start.4 = ((s8[21233664]{0:T(1024)(128)(4,1)}), s8[4194304]{0:T(1024)(128)(4,1)S(1)}, s32[]{:S(2)}) async-start(s8[21233664]{0:T(1024)(128)(4,1)} %bitcast.268), calls=%async_computation.12 | async-start | bytes 8388608 | tf_op jit(solution)/shard_map/while
  487.5 26.8 %slice-start.5 = ((s8[21233664]{0:T(1024)(128)(4,1)}), s8[262144]{0:T(1024)(128)(4,1)S(1)}, s32[]{:S(2)}) async-start(s8[21233664]{0:T(1024)(128)(4,1)} %bitcast.268), calls=%async_computation.13 | async-start | bytes 524288 | tf_op jit(solution)/shard_map/while
  537.6 76.3 %copy-start = (bf16[2,256,1152]{2,1,0:T(8,128)(2,1)S(1)}, bf16[2,256,1152]{2,1,0:T(8,128)(2,1)}, u32[]{:S(2)}) copy-start(bf16[2,256,1152]{2,1,0:T(8,128)(2,1)} %get-tuple-element.1049) | copy-start | bytes 3538948 | tf_op jit(solution)/shard_map/while
  612.5 51.7 %collective-permute-start.1 = (bf16[256,1152]{1,0:T(8,128)(2,1)}, bf16[256,1152]{1,0:T(8,128)(2,1)}, u32[]{:S(2)}, u32[]{:S(2)}) collective-permute-start(bf16[256,1152]{1,0:T(8,128)(2,1)} %get-tuple-element.935), channel_id=1, source_target_pairs={{1,0},{2,1},{3,2},{5,4},{6,5},{7,6},{9,8},{10,9},{11,10},{13,12},{... | collective-permute-start | bytes 1769480 | tf_op jit(solution)/shard_map/while/body/eval_jaxpr/ppermute | solution.py:26
  618.1 22.6 %slice-start.1 = ((s8[21233664]{0:T(1024)(128)(4,1)}), s8[4194304]{0:T(1024)(128)(4,1)S(1)}, s32[]{:S(2)}) async-start(s8[21233664]{0:T(1024)(128)(4,1)} %bitcast.268), calls=%async_computation.9 | async-start | bytes 8388608 | tf_op jit(solution)/shard_map/while
  618.1 24.5 %slice-start.2 = ((s8[21233664]{0:T(1024)(128)(4,1)}), s8[4194304]{0:T(1024)(128)(4,1)S(1)}, s32[]{:S(2)}) async-start(s8[21233664]{0:T(1024)(128)(4,1)} %bitcast.268), calls=%async_computation.10 | async-start | bytes 8388608 | tf_op jit(solution)/shard_map/while
  618.1 25.7 %slice-start.3 = ((s8[21233664]{0:T(1024)(128)(4,1)}), s8[4194304]{0:T(1024)(128)(4,1)S(1)}, s32[]{:S(2)}) async-start(s8[21233664]{0:T(1024)(128)(4,1)} %bitcast.268), calls=%async_computation.11 | async-start | bytes 8388608 | tf_op jit(solution)/shard_map/while
  618.1 26.9 %slice-start.4 = ((s8[21233664]{0:T(1024)(128)(4,1)}), s8[4194304]{0:T(1024)(128)(4,1)S(1)}, s32[]{:S(2)}) async-start(s8[21233664]{0:T(1024)(128)(4,1)} %bitcast.268), calls=%async_computation.12 | async-start | bytes 8388608 | tf_op jit(solution)/shard_map/while
  618.2 26.8 %slice-start.5 = ((s8[21233664]{0:T(1024)(128)(4,1)}), s8[262144]{0:T(1024)(128)(4,1)S(1)}, s32[]{:S(2)}) async-start(s8[21233664]{0:T(1024)(128)(4,1)} %bitcast.268), calls=%async_computation.13 | async-start | bytes 524288 | tf_op jit(solution)/shard_map/while
  669.5 75.9 %copy-start = (bf16[2,256,1152]{2,1,0:T(8,128)(2,1)S(1)}, bf16[2,256,1152]{2,1,0:T(8,128)(2,1)}, u32[]{:S(2)}) copy-start(bf16[2,256,1152]{2,1,0:T(8,128)(2,1)} %get-tuple-element.1049) | copy-start | bytes 3538948 | tf_op jit(solution)/shard_map/while
  744.1 51.7 %collective-permute-start.1 = (bf16[256,1152]{1,0:T(8,128)(2,1)}, bf16[256,1152]{1,0:T(8,128)(2,1)}, u32[]{:S(2)}, u32[]{:S(2)}) collective-permute-start(bf16[256,1152]{1,0:T(8,128)(2,1)} %get-tuple-element.935), channel_id=1, source_target_pairs={{1,0},{2,1},{3,2},{5,4},{6,5},{7,6},{9,8},{10,9},{11,10},{13,12},{... | collective-permute-start | bytes 1769480 | tf_op jit(solution)/shard_map/while/body/eval_jaxpr/ppermute | solution.py:26
  749.7 22.6 %slice-start.1 = ((s8[21233664]{0:T(1024)(128)(4,1)}), s8[4194304]{0:T(1024)(128)(4,1)S(1)}, s32[]{:S(2)}) async-start(s8[21233664]{0:T(1024)(128)(4,1)} %bitcast.268), calls=%async_computation.9 | async-start | bytes 8388608 | tf_op jit(solution)/shard_map/while
  749.7 24.5 %slice-start.2 = ((s8[21233664]{0:T(1024)(128)(4,1)}), s8[4194304]{0:T(1024)(128)(4,1)S(1)}, s32[]{:S(2)}) async-start(s8[21233664]{0:T(1024)(128)(4,1)} %bitcast.268), calls=%async_computation.10 | async-start | bytes 8388608 | tf_op jit(solution)/shard_map/while
  749.7 25.7 %slice-start.3 = ((s8[21233664]{0:T(1024)(128)(4,1)}), s8[4194304]{0:T(1024)(128)(4,1)S(1)}, s32[]{:S(2)}) async-start(s8[21233664]{0:T(1024)(128)(4,1)} %bitcast.268), calls=%async_computation.11 | async-start | bytes 8388608 | tf_op jit(solution)/shard_map/while
  749.7 26.9 %slice-start.4 = ((s8[21233664]{0:T(1024)(128)(4,1)}), s8[4194304]{0:T(1024)(128)(4,1)S(1)}, s32[]{:S(2)}) async-start(s8[21233664]{0:T(1024)(128)(4,1)} %bitcast.268), calls=%async_computation.12 | async-start | bytes 8388608 | tf_op jit(solution)/shard_map/while
  749.7 26.8 %slice-start.5 = ((s8[21233664]{0:T(1024)(128)(4,1)}), s8[262144]{0:T(1024)(128)(4,1)S(1)}, s32[]{:S(2)}) async-start(s8[21233664]{0:T(1024)(128)(4,1)} %bitcast.268), calls=%async_computation.13 | async-start | bytes 524288 | tf_op jit(solution)/shard_map/while
  853.4 467.9 %all-reduce.4.cloned.1.call-start = ((), (), s32[]{:S(2)}) async-start(), calls=%async_computation.6 | async-start | bytes 15925248 | tf_op jit(solution)/shard_map/psum | solution.py:412
  862.7 645.8 %reduce-scatter.5.cloned.1.call-start = ((), (), s32[]{:S(2)}) async-start(), calls=%async_computation.5 | async-start | bytes 10948608 | tf_op jit(solution)/shard_map/reduce_scatter | solution.py:400
  875.0 818.1 %reduce-scatter.3.cloned.1.call-start = ((), (), s32[]{:S(2)}) async-start(), calls=%async_computation.4 | async-start | bytes 10948608 | tf_op jit(solution)/shard_map/reduce_scatter | solution.py:397
  (102 other events, 717.0 us)
Sparse Core Ops, SparseCore 0:
  10.3 29.5 all-gather.2
  42.1 27.5 all-gather.4
  853.5 122.8 all-reduce.5
  979.4 341.8 all-reduce.3
  1323.7 184.7 reduce-scatter.4
  1510.9 182.1 reduce-scatter.2
where the time goes:
time: 1710 us; the launch traced here: 1700 us
  waiting for transfers between devices  667 us (39%)
  other arithmetic  305 us (18%)
  local copies, waits for them, and re-layouts  257 us (15%)
  blocking collectives  161 us (9%)
  loops' own time  135 us (8%)
  matrix products  91.2 us (5%)
  starting transfers between devices  71.4 us (4%)
    psum x1, waiting for transfers between devices, local(): lax.psum(local_product.astype(jnp.bfloat16), 'dp').astype(jnp.float32)  264 us
    reduce_scatter x1, waiting for transfers between devices, local(): lax.psum_scatter(first_total.astype(jnp.bfloat16), 'dp', scatter_dimensio...  183 us
    reduce_scatter x1, waiting for transfers between devices, local(): lax.psum_scatter(second_total.astype(jnp.bfloat16), 'dp', scatter_dimensi...  177 us
    psum x1, blocking collectives, local(): lax.psum(jnp.sum(modulation_grads, axis=0).astype(jnp.bfloat16), 'dp')  161 us
    another operation x5, loops' own time, backward_tick(): lax.switch(chosen_section, backward_sections, stash_rows[micro_index], up...  115 us
    add x5, other arithmetic, backward_tick(): first_total = first_total + first_part  108 us
    another operation x16, local copies, waits for them, and re-layouts  74.7 us
    add x5, other arithmetic, backward_tick(): second_total = second_total + second_part  74 us
  transfers between devices with their start and end apart: 16, of which 10 were waited for; matrix products, arithmetic and copies ran while one was open for 17% of the time, Pallas kernels for 0%

commit v1 on v0

v1 whole, which is shorter than its diff:
```python
import functools
import math

import jax
import jax.numpy as jnp
from jax import lax
from jax.experimental import pallas as pl
from jax.experimental.pallas import tpu as pltpu
from jax.sharding import PartitionSpec as P

HEADS = 16
SIDE = 20
SLOTS = SIDE * SIDE
VALID = 256
KEPT = 128
D = 1152
FF = 4608
HALF = FF // 2
QUARTER = D // 4
HEAD = D // HEADS
BLOCK = FF // 32
EPSILON = 1e-06
FACTOR = 1.0 / math.sqrt(HEAD)
LOG2E = math.log2(math.e)
NEGATIVE = -1e30
BF = jnp.bfloat16
F32 = jnp.float32
VMEM = pltpu.VMEM
MESH = pl.DeviceIdType.MESH
NT = (((1,), (1,)), ((), ()))
TN = (((0,), (0,)), ((), ()))
C0 = math.sqrt(2.0 / math.pi)


def mm(a, b, dims=(((1,), (0,)), ((), ()))):
    return lax.dot_general(a, b, dims, preferred_element_type=F32)


def params(mb=50):
    return pltpu.CompilerParams(vmem_limit_bytes=mb * 2**20)


def whole(shape):
    return pl.BlockSpec(shape, lambda *_: (0,) * len(shape))


def cost(flops, nbytes):
    return pl.CostEstimate(flops=int(flops), bytes_accessed=int(nbytes), transcendentals=0)


def array(*shape, dtype=BF):
    return jax.ShapeDtypeStruct(shape, dtype)


def norm_stats(x):
    mean = jnp.mean(x, axis=-1, keepdims=True)
    centred = x - mean
    rstd = lax.rsqrt(jnp.mean(centred * centred, axis=-1, keepdims=True) + EPSILON)
    return centred * rstd, rstd


def hidden_of(rows_ref, mod_ref):
    normed, _ = norm_stats(rows_ref[...].astype(F32))
    return (normed * (1.0 + mod_ref[1:2, :]) + mod_ref[0:1, :]).astype(BF)


def norm_backward(rows, mod_ref, upstream, hidden_grad, modgrad_ref):
    normed, rstd = norm_stats(rows)
    modgrad_ref[0:1, :] = jnp.sum(hidden_grad, axis=0, keepdims=True)
    modgrad_ref[1:2, :] = jnp.sum(hidden_grad * normed, axis=0, keepdims=True)
    scaled = hidden_grad * (1.0 + mod_ref[1:2, :])
    mean_scaled = jnp.mean(scaled, axis=-1, keepdims=True)
    mean_product = jnp.mean(scaled * normed, axis=-1, keepdims=True)
    return upstream + (scaled - mean_scaled - normed * mean_product) * rstd


def gelu_pair(v):
    square = v * v
    t = jnp.tanh(v * (C0 + (C0 * 0.044715) * square))
    half = 0.5 * (1.0 + t)
    slope = half + (0.5 * v) * (1.0 - t * t) * (C0 + (3.0 * C0 * 0.044715) * square)
    return v * half, slope


def pick_kept(rows, kept_col):
    lane = lax.broadcasted_iota(jnp.int32, (KEPT, VALID), 1)
    return mm((lane == kept_col).astype(BF), rows).astype(BF)


def merge_kept(base, kept_rows, kept_row):
    line = lax.broadcasted_iota(jnp.int32, (VALID, KEPT), 0)
    spread = (line == kept_row).astype(F32)
    chosen = jnp.sum(spread, axis=1, keepdims=True) > 0.5
    return jnp.where(chosen, mm(spread.astype(BF), kept_rows).astype(BF), base)


def windows():
    for head in range(HEADS):
        first = head * HEAD
        start = first // 128 * 128
        stop = (first + HEAD - 1) // 128 * 128 + 128
        yield start, stop - start, first - start


def only_head(value, offset):
    lane = lax.broadcasted_iota(jnp.int32, value.shape, 1)
    return jnp.where((lane >= offset) & (lane < offset + HEAD), value, jnp.zeros_like(value))


def key_bias(live_ref, keys):
    lane = lax.broadcasted_iota(jnp.int32, (1, keys), 1)
    return jnp.where(lane < live_ref[0], 0.0, NEGATIVE).astype(F32)


def softmax_of(q, k, bias):
    scores = mm(q, k, NT) + bias
    top = jnp.max(scores, axis=-1, keepdims=True)
    grown = jnp.exp2((scores - top) * (FACTOR * LOG2E))
    return grown * (1.0 / jnp.sum(grown, axis=-1, keepdims=True))


def attention_forward_kernel(
    live_ref, rows_ref, mod_ref, w_ref, out_ref, hidden_ref, joined_ref, branch_ref, proj, mixed
):
    step = pl.program_id(0)

    @pl.when(step == 0)
    def _():
        hidden_ref[...] = hidden_of(rows_ref, mod_ref)

    @pl.when(step < 3)
    def _():
        part = mm(hidden_ref[...], w_ref[...]).astype(BF)
        proj[step] = part
        joined_ref[...] = part

    @pl.when(step == 3)
    def _():
        bias = key_bias(live_ref, rows_ref.shape[0])
        mixed[...] = jnp.zeros_like(mixed)
        for start, width, offset in windows():
            cut = pl.ds(start, width)
            q = only_head(proj[0, :, cut], offset)
            v = only_head(proj[2, :, cut], offset)
            soft = softmax_of(q, proj[1, :, cut], bias).astype(BF)
            mixed[:, cut] += mm(soft, v)
        mixed_low = mixed[...].astype(BF)
        joined_ref[...] = mixed_low
        branch = mm(mixed_low, w_ref[...])
        branch_ref[...] = branch.astype(BF)
        out_ref[...] = (rows_ref[...].astype(F32) + mod_ref[2:3, :] * branch).astype(BF)


def attention_forward(r, live, rows, mod, weights):
    row = pl.BlockSpec((r, D), lambda j: (0, 0))
    return pl.pallas_call(
        attention_forward_kernel,
        grid=(4,),
        in_specs=[
            pl.BlockSpec(memory_space=pltpu.SMEM),
            row,
            whole((3, D)),
            pl.BlockSpec((D, D), lambda j: (0, j)),
        ],
        out_specs=[row, row, pl.BlockSpec((r, D), lambda j: (0, j)), row],
        out_shape=(array(VALID, D), array(VALID, D), array(VALID, FF), array(VALID, D)),
        scratch_shapes=[VMEM((3, r, D), BF), VMEM((r, D), F32)],
        compiler_params=params(),
        cost_estimate=cost(2 * r * D * FF, 2 * D * FF),
        name="attention_forward",
    )(live, rows, mod, weights)


def attention_backward_kernel(
    live_ref, rows_ref, mod_ref, w_ref, joined_ref, branch_ref, up_ref,
    grad_ref, kept_ref, sent_ref, modgrad_ref, parts, pg, bg_keep, hidden_grad,
):
    step = pl.program_id(0)

    @pl.when(step == 0)
    def _():
        up = up_ref[...].astype(F32)
        modgrad_ref[2:3, :] = jnp.sum(up * branch_ref[...].astype(F32), axis=0, keepdims=True)
        bg = (up * mod_ref[2:3, :]).astype(BF)
        bg_keep[...] = bg
        mixed_grad = mm(bg, w_ref[...], NT).astype(BF)
        bias = key_bias(live_ref, rows_ref.shape[0])
        parts[...] = jnp.zeros_like(parts)
        for start, width, offset in windows():
            cut = pl.ds(start, width)
            q = only_head(joined_ref[:, pl.ds(start, width)], offset)
            k = only_head(joined_ref[:, pl.ds(D + start, width)], offset)
            v = joined_ref[:, pl.ds(2 * D + start, width)]
            mg = only_head(mixed_grad[:, start : start + width], offset)
            soft = softmax_of(q, k, bias)
            soft_grad = mm(mg, v, NT)
            parts[2, :, cut] += mm(soft.astype(BF), mg, TN)
            product = soft * soft_grad
            total = jnp.sum(product, axis=-1, keepdims=True)
            score_grad = (product - soft * total).astype(BF)
            parts[0, :, cut] += mm(score_grad, k)
            parts[1, :, cut] += mm(score_grad, q, TN)
        pg[0] = (parts[0] * FACTOR).astype(BF)
        pg[1] = (parts[1] * FACTOR).astype(BF)
        pg[2] = parts[2].astype(BF)
        low = live_ref[1] == 0

        @pl.when(low)
        def _():
            kept_ref[0] = pg[0]
            kept_ref[1] = pg[1]
            sent_ref[0] = pg[2]
            sent_ref[1] = bg_keep[...]

        @pl.when(jnp.logical_not(low))
        def _():
            sent_ref[0] = pg[0]
            sent_ref[1] = pg[1]
            kept_ref[0] = pg[2]
            kept_ref[1] = bg_keep[...]

    @pl.when(step > 0)
    def _():
        part = mm(pg[step - 1], w_ref[...], NT)

        @pl.when(step == 1)
        def _():
            hidden_grad[...] = part

        @pl.when(step > 1)
        def _():
            hidden_grad[...] += part

    @pl.when(step == 3)
    def _():
        grad = norm_backward(
            rows_ref[...].astype(F32), mod_ref, up_ref[...].astype(F32), hidden_grad[...], modgrad_ref
        )
        grad_ref[...] = grad.astype(BF)


def attention_backward(r, live, rows, mod, weights, joined, branch, up):
    row = pl.BlockSpec((r, D), lambda j: (0, 0))
    pair = pl.BlockSpec((2, r, D), lambda j: (0, 0, 0))
    return pl.pallas_call(
        attention_backward_kernel,
        grid=(4,),
        in_specs=[
            pl.BlockSpec(memory_space=pltpu.SMEM),
            row,
            whole((3, D)),
            pl.BlockSpec((D, D), lambda j: (0, (j + 3) % 4)),
            pl.BlockSpec((r, 3 * D), lambda j: (0, 0)),
            row,
            row,
        ],
        out_specs=[row, pair, pair, whole((3, D))],
        out_shape=(array(VALID, D), array(2, VALID, D), array(2, VALID, D), array(3, D, dtype=F32)),
        scratch_shapes=[VMEM((3, r, D), F32), VMEM((3, r, D), BF), VMEM((r, D), BF), VMEM((r, D), F32)],
        compiler_params=params(),
        cost_estimate=cost(2 * r * D * FF, 2 * D * FF),
        name="attention_backward",
    )(live, rows, mod, weights, joined, branch, up)


def attention_weights_kernel(low_ref, *refs):
    lefts, hiddens, mixeds, out_ref = refs[0:4], refs[4:8], refs[8:12], refs[12]
    use_mixed = (low_ref[0] == 1) & (pl.program_id(0) == 1)

    def total(rights):
        parts = [mm(a[0], b[...], TN) for a, b in zip(lefts, rights)]
        out_ref[...] = sum(parts[1:], parts[0]).astype(BF)

    @pl.when(use_mixed)
    def _():
        total(mixeds)

    @pl.when(jnp.logical_not(use_mixed))
    def _():
        total(hiddens)


def attention_weights(r, low, lefts, hiddens, own_joined, other_mixed, chunk=384):
    left = pl.BlockSpec((1, r, chunk), lambda p, j, low: (p, 0, j))
    row = pl.BlockSpec((r, D), lambda p, j, low: (0, 0))
    joined = pl.BlockSpec((r, D), lambda p, j, low: (0, 3))
    per = D // chunk
    return pl.pallas_call(
        attention_weights_kernel,
        grid_spec=pltpu.PrefetchScalarGridSpec(
            num_scalar_prefetch=1,
            grid=(2, per),
            in_specs=[left] * 4 + [row] * 4 + [joined] * 2 + [row] * 2,
            out_specs=pl.BlockSpec((chunk, D), lambda p, j, low: (p * per + j, 0)),
        ),
        out_shape=array(HALF, D),
        compiler_params=params(),
        cost_estimate=cost(8 * r * D * HALF, 2 * D * HALF),
        name="attention_weights",
    )(low, *lefts, *hiddens, *own_joined, *other_mixed)


def feed_forward_kernel(
    rows_ref, mod_ref, w1_ref, w2_ref, kept_ref, out_ref, hidden_ref, active_ref, slope_ref, branch_ref, picked_ref, total
):
    step = pl.program_id(0)

    @pl.when(step == 0)
    def _():
        hidden_ref[...] = hidden_of(rows_ref, mod_ref)

    active, slope = gelu_pair(mm(hidden_ref[...], w1_ref[...]))
    active_low = active.astype(BF)
    active_ref[...] = active_low
    slope_ref[...] = slope.astype(BF)
    part = mm(active_low, w2_ref[...])

    @pl.when(step == 0)
    def _():
        total[...] = part

    @pl.when(step > 0)
    def _():
        total[...] += part

    @pl.when(step == pl.num_programs(0) - 1)
    def _():
        branch = total[...]
        branch_ref[...] = branch.astype(BF)
        out = (rows_ref[...].astype(F32) + mod_ref[2:3, :] * branch).astype(BF)
        out_ref[...] = out
        picked_ref[...] = pick_kept(out, kept_ref[...])


def feed_forward(rows, mod, w1, w2, kept_col, chunk=1152):
    r = VALID
    low = array(r, D)
    big = array(r, FF)
    col = pl.BlockSpec((r, chunk), lambda j: (0, j))
    return pl.pallas_call(
        feed_forward_kernel,
        grid=(FF // chunk,),
        in_specs=[
            whole((r, D)),
            whole((3, D)),
            pl.BlockSpec((D, chunk), lambda j: (0, j)),
            pl.BlockSpec((chunk, D), lambda j: (j, 0)),
            whole((KEPT, 1)),
        ],
        out_specs=[whole((r, D)), whole((r, D)), col, col, whole((r, D)), whole((KEPT, D))],
        out_shape=(low, low, big, big, low, array(KEPT, D)),
        scratch_shapes=[VMEM((r, D), F32)],
        compiler_params=params(),
        cost_estimate=cost(4 * r * D * FF, 4 * D * FF),
        name="feed_forward",
    )(rows, mod, w1, w2, kept_col)


def feed_backward_kernel(
    rows_ref, mod_ref, w1_ref, w2_ref, slope_ref, branch_ref, base_ref, picked_ref, kept_ref,
    grad_ref, bg_ref, ig_ref, modgrad_ref, total, up_low,
):
    step = pl.program_id(0)

    @pl.when(step == 0)
    def _():
        low = merge_kept(base_ref[...], picked_ref[...], kept_ref[...])
        up_low[...] = low
        up = low.astype(F32)
        modgrad_ref[2:3, :] = jnp.sum(up * branch_ref[...].astype(F32), axis=0, keepdims=True)
        bg_ref[...] = (up * mod_ref[2:3, :]).astype(BF)

    active_grad = mm(bg_ref[...], w2_ref[...], NT)
    inner_grad = (active_grad * slope_ref[...].astype(F32)).astype(BF)
    ig_ref[...] = inner_grad
    part = mm(inner_grad, w1_ref[...], NT)

    @pl.when(step == 0)
    def _():
        total[...] = part

    @pl.when(step > 0)
    def _():
        total[...] += part

    @pl.when(step == pl.num_programs(0) - 1)
    def _():
        grad = norm_backward(
            rows_ref[...].astype(F32), mod_ref, up_low[...].astype(F32), total[...], modgrad_ref
        )
        grad_ref[...] = grad.astype(BF)


def feed_backward(rows, mod, w1, w2, slope, branch, base, picked, kept_row, chunk=1152):
    r = VALID
    low = array(r, D)
    col = pl.BlockSpec((r, chunk), lambda j: (0, j))
    return pl.pallas_call(
        feed_backward_kernel,
        grid=(FF // chunk,),
        in_specs=[
            whole((r, D)),
            whole((3, D)),
            pl.BlockSpec((D, chunk), lambda j: (0, j)),
            pl.BlockSpec((chunk, D), lambda j: (j, 0)),
            col,
            whole((r, D)),
            whole((r, D)),
            whole((KEPT, D)),
            whole((1, KEPT)),
        ],
        out_specs=[whole((r, D)), whole((r, D)), col, whole((3, D))],
        out_shape=(low, low, array(r, FF), array(3, D, dtype=F32)),
        scratch_shapes=[VMEM((r, D), F32), VMEM((r, D), BF)],
        compiler_params=params(),
        cost_estimate=cost(4 * r * D * FF, 4 * D * FF),
        name="feed_backward",
    )(rows, mod, w1, w2, slope, branch, base, picked, kept_row)


def feed_both_kernel(
    rows_ref, mod_ref, w1_ref, w2_ref, up_ref,
    out_ref, hidden_ref, active_ref, grad_ref, bg_ref, ig_ref, modgrad_ref, total, back,
):
    step = pl.program_id(0)

    @pl.when(step == 0)
    def _():
        hidden_ref[...] = hidden_of(rows_ref, mod_ref)
        bg_ref[...] = (up_ref[...].astype(F32) * mod_ref[2:3, :]).astype(BF)
        total[...] = jnp.zeros_like(total)
        back[...] = jnp.zeros_like(back)

    inner = mm(hidden_ref[...], w1_ref[...])
    active_grad = mm(bg_ref[...], w2_ref[...], NT)
    active, slope = gelu_pair(inner)
    active_low = active.astype(BF)
    active_ref[...] = active_low
    inner_grad = (active_grad * slope).astype(BF)
    ig_ref[...] = inner_grad
    total[...] += mm(active_low, w2_ref[...])
    back[...] += mm(inner_grad, w1_ref[...], NT)

    @pl.when(step == pl.num_programs(0) - 1)
    def _():
        branch = total[...]
        rows = rows_ref[...].astype(F32)
        up = up_ref[...].astype(F32)
        out_ref[...] = (rows + mod_ref[2:3, :] * branch).astype(BF)
        modgrad_ref[2:3, :] = jnp.sum(up * branch, axis=0, keepdims=True)
        grad = norm_backward(rows, mod_ref, up, back[...], modgrad_ref)
        grad_ref[...] = grad.astype(BF)


def feed_both(rows, mod, w1, w2, up, chunk=768):
    r = KEPT
    row = pl.BlockSpec((r, D), lambda j: (0, 0))
    col = pl.BlockSpec((r, chunk), lambda j: (0, j))
    low = array(VALID, D)
    big = array(VALID, FF)
    return pl.pallas_call(
        feed_both_kernel,
        grid=(FF // chunk,),
        in_specs=[
            row,
            whole((3, D)),
            pl.BlockSpec((D, chunk), lambda j: (0, j)),
            pl.BlockSpec((chunk, D), lambda j: (j, 0)),
            row,
        ],
        out_specs=[row, row, col, row, row, col, whole((3, D))],
        out_shape=(low, low, big, low, low, big, array(3, D, dtype=F32)),
        scratch_shapes=[VMEM((r, D), F32), VMEM((r, D), F32)],
        compiler_params=params(),
        cost_estimate=cost(8 * r * D * FF, 4 * D * FF),
        name="feed_both",
    )(rows, mod, w1, w2, up)


def feed_weights_kernel(low_ref, *refs):
    hid_own, hid_other, bg_own, bg_other = refs[0:2], refs[2:4], refs[4:6], refs[6:8]
    active_own, ig_own = refs[8:10], refs[10:12]
    w1_ref, w2_ref, first_ref, second_ref = refs[12:16]
    first = second = None
    for c in range(2):
        part = mm(ig_own[c][...], hid_own[c][...], TN)
        first = part if first is None else first + part
        part = mm(active_own[c][...], bg_own[c][...], TN)
        second = part if second is None else second + part
    for c in range(2):
        hidden, bg = hid_other[c][...], bg_other[c][...]
        active, slope = gelu_pair(mm(hidden, w1_ref[...]))
        inner_grad = mm(bg, w2_ref[...], NT) * slope
        first = first + mm(inner_grad.astype(BF), hidden, TN)
        second = second + mm(active.astype(BF), bg, TN)
    first_ref[...] = first.astype(BF)
    second_ref[...] = second.astype(BF)


def feed_weights(r, low, hid_own, hid_other, bg_own, bg_other, active_own, ig_own, w1, w2, chunk=384):
    per = HALF // chunk
    row = pl.BlockSpec((r, D), lambda j, low: (0, 0))
    col = pl.BlockSpec((r, chunk), lambda j, low: (0, low[0] * per + j))
    out = pl.BlockSpec((chunk, D), lambda j, low: (j, 0))
    return pl.pallas_call(
        feed_weights_kernel,
        grid_spec=pltpu.PrefetchScalarGridSpec(
            num_scalar_prefetch=1,
            grid=(per,),
            in_specs=[row] * 8
            + [col] * 4
            + [
                pl.BlockSpec((D, chunk), lambda j, low: (0, low[0] * per + j)),
                pl.BlockSpec((chunk, D), lambda j, low: (low[0] * per + j, 0)),
            ],
            out_specs=[out, out],
        ),
        out_shape=(array(HALF, D), array(HALF, D)),
        compiler_params=params(),
        cost_estimate=cost(24 * r * D * HALF, 8 * D * HALF),
        name="feed_weights",
    )(low, *hid_own, *hid_other, *bg_own, *bg_other, *active_own, *ig_own, w1, w2)


def move_rows_kernel(count, refs):
    index_ref = refs[0]
    for i in range(count):
        source, target = refs[1 + i], refs[1 + count + i]
        for c in range(source.shape[0]):
            index = index_ref[c]
            lane = lax.broadcasted_iota(jnp.int32, (index.shape[0], source.shape[1]), 1)
            target[c] = mm((lane == index).astype(BF), source[c]).astype(BF)


def move_rows(index, *sources):
    count = len(sources)
    rows = index.shape[1]
    spec = pl.BlockSpec(memory_space=VMEM)
    return pl.pallas_call(
        lambda *refs: move_rows_kernel(count, refs),
        in_specs=[spec] * (1 + count),
        out_specs=[spec] * count,
        out_shape=[array(s.shape[0], rows, s.shape[2]) for s in sources],
        compiler_params=params(),
        name="move_rows",
    )(index, *sources)


def merge_kernel(base_ref, kept_ref, index_ref, out_ref):
    out_ref[...] = merge_kept(base_ref[...], kept_ref[...], index_ref[...])


def merge(base, kept, kept_row):
    return pl.pallas_call(
        merge_kernel,
        grid=(1,),
        in_specs=[whole((VALID, D)), pl.BlockSpec((KEPT, D), lambda j: (0, 0)), whole((1, KEPT))],
        out_specs=whole((VALID, D)),
        out_shape=array(VALID, D),
        compiler_params=params(),
        name="merge_kept",
    )(base, kept, kept_row)


def unwritten(*shapes):
    spec = pl.BlockSpec(memory_space=pl.ANY)
    return pl.pallas_call(lambda *refs: None, out_specs=[spec] * len(shapes), out_shape=list(shapes), name="unwritten")()


FLOWS = ((0, "y", 0, 640), (0, "z", 640, 512), (1, "y", 0, 512), (1, "z", 512, 640))
CUT = 80


def sum_kernel(first_ref, second_ref, first_out, second_out, *scratch):
    count = len(FLOWS)
    per = 6
    ones, twos, threes, sums, tiny1, tiny2, tiny3 = (scratch[i * count : (i + 1) * count] for i in range(7))
    ends = scratch[7 * count]
    arrive = scratch[7 * count + 1]
    dp, section = lax.axis_index("dp"), lax.axis_index("section")
    x, z, y = dp // 16, (dp // 4) % 4, dp % 4
    place = {"y": y, "z": z}

    def neighbour(axis, by):
        if axis == "y":
            return (x * 16 + z * 4 + (y + by) % 4, section)
        return (x * 16 + ((z + by) % 4) * 4 + y, section)

    barrier = pltpu.get_barrier_semaphore()
    for axis in ("y", "z"):
        for by in (1, 3):
            pl.semaphore_signal(barrier, inc=1, device_id=neighbour(axis, by), device_id_type=MESH)
    pl.semaphore_wait(barrier, 4)

    data = (first_ref, second_ref)
    outs = (first_out, second_out)

    def copy(flow, phase, kind, side, source, target):
        axis = FLOWS[flow][1]
        if phase == 1:
            axis = "z" if axis == "y" else "y"
        number = ((flow * 2 + phase) * 3 + kind) * 2 + side
        return pltpu.make_async_remote_copy(
            src_ref=source,
            dst_ref=target,
            send_sem=ends.at[number],
            recv_sem=arrive.at[number],
            device_id=neighbour(axis, 1 if side == 0 else 3),
            device_id_type=MESH,
        )

    halves = (pl.ds(0, 2), pl.ds(2, 2))
    cuts = (pl.ds(0, CUT), pl.ds(CUT, BLOCK - CUT))

    def block(flow, position, part):
        which, axis, low, width = FLOWS[flow]
        columns = pl.ds(low, width)
        if axis == "y":
            return data[which].at[part, position, :, columns]
        return data[which].at[position, part, :, columns]

    pending = {}

    def start(flow, phase, kind, side, build):
        pending[(flow, phase, kind, side)] = lambda: copy(flow, phase, kind, side, *build())
        pending[(flow, phase, kind, side)]().start()

    def begin(flow):
        for side in (0, 1):
            start(flow, 0, 0, side, lambda side=side: (block(flow, (place[FLOWS[flow][1]] + 2) % 4, halves[side]), ones[flow].at[side]))
        for side in (0, 1):
            start(flow, 0, 1, side, lambda side=side: (block(flow, (place[FLOWS[flow][1]] + (1, 3)[side]) % 4, halves[1 - side]), twos[flow].at[side]))

    def forward(flow):
        at = place[FLOWS[flow][1]]
        for side in (0, 1):
            pending[(flow, 0, 0, side)]().wait()
            own = block(flow, (at + (1, 3)[side]) % 4, halves[side])[...]
            ones[flow][side] = (ones[flow][side].astype(F32) + own.astype(F32)).astype(BF)
            start(flow, 0, 2, side, lambda side=side: (ones[flow].at[side], threes[flow].at[side]))

    def middle(flow):
        at = place[FLOWS[flow][1]]
        for side in (0, 1):
            pending[(flow, 0, 1, side)]().wait()
            pending[(flow, 0, 2, side)]().wait()
        for half in (0, 1):
            own = block(flow, at, halves[half])[...].astype(F32)
            total = own + threes[flow][half].astype(F32) + twos[flow][1 - half].astype(F32)
            sums[flow][halves[half]] = total.astype(BF)

        def slab(by, cut):
            second = place["z" if FLOWS[flow][1] == "y" else "y"]
            return sums[flow].at[(second + by) % 4, cut]

        for side in (0, 1):
            start(flow, 1, 0, side, lambda side=side: (slab(2, cuts[side]), tiny1[flow].at[cuts[side]]))
        for side in (0, 1):
            start(flow, 1, 1, side, lambda side=side: (slab((1, 3)[side], cuts[1 - side]), tiny2[flow].at[cuts[1 - side]]))

    def late(flow):
        second = place["z" if FLOWS[flow][1] == "y" else "y"]
        for side in (0, 1):
            pending[(flow, 1, 0, side)]().wait()
            own = sums[flow][(second + (1, 3)[side]) % 4, cuts[side]]
            tiny1[flow][cuts[side]] = (tiny1[flow][cuts[side]].astype(F32) + own.astype(F32)).astype(BF)
            start(flow, 1, 2, side, lambda side=side: (tiny1[flow].at[cuts[side]], tiny3[flow].at[cuts[side]]))

    def finish(flow):
        which, axis, low, width = FLOWS[flow]
        second = place["z" if axis == "y" else "y"]
        for side in (0, 1):
            pending[(flow, 1, 1, side)]().wait()
            pending[(flow, 1, 2, side)]().wait()
        total = sums[flow][second].astype(F32) + tiny2[flow][...].astype(F32) + tiny3[flow][...].astype(F32)
        outs[which][:, low : low + width] = total

    even = [i for i, f in enumerate(FLOWS) if f[0] == 0]
    odd = [i for i, f in enumerate(FLOWS) if f[0] == 1]
    is_odd = section % 2 == 1

    @pl.when(jnp.logical_not(is_odd))
    def _():
        second_out[...] = jnp.zeros_like(second_out)

    for stage in (begin, forward, middle, late, finish):
        for flow in even:
            stage(flow)

        @pl.when(is_odd)
        def _():
            for flow in odd:
                stage(flow)


def sum_blocks(first, second):
    spec = pl.BlockSpec(memory_space=VMEM)
    widths = [f[3] for f in FLOWS]
    count = len(FLOWS)
    pair = [VMEM((2, 2, BLOCK, w), BF) for w in widths]
    tiny = [VMEM((BLOCK, w), BF) for w in widths]
    return pl.pallas_call(
        sum_kernel,
        in_specs=[spec] * 2,
        out_specs=[spec] * 2,
        out_shape=[array(BLOCK, D, dtype=F32)] * 2,
        scratch_shapes=pair * 3
        + [VMEM((4, BLOCK, w), BF) for w in widths]
        + tiny * 3
        + [pltpu.SemaphoreType.DMA((count * 12,)), pltpu.SemaphoreType.DMA((count * 12,))],
        compiler_params=pltpu.CompilerParams(
            collective_id=0, has_side_effects=True, vmem_limit_bytes=56 * 2**20
        ),
        cost_estimate=cost(FF * D, 4 * FF * D),
        name="sum_blocks",
    )(first.reshape(4, 4, BLOCK, D), second.reshape(4, 4, BLOCK, D))


def canvas_layout(shape_id):
    grid_rows = jnp.where(shape_id == 1, 12, jnp.where(shape_id == 2, 20, 16)).astype(jnp.int32)
    grid_width = jnp.where(shape_id == 1, 20, jnp.where(shape_id == 2, 12, 16)).astype(jnp.int32)
    token = jnp.arange(VALID, dtype=jnp.int32)
    live = grid_rows * grid_width
    token_slot = jnp.where(token < live, token // grid_width * SIDE + token % grid_width, -1)
    slot = jnp.arange(SLOTS, dtype=jnp.int32)
    line, column = slot // SIDE, slot % SIDE
    filled = (line < grid_rows) & (column < grid_width)
    slot_token = jnp.where(filled, line * grid_width + column, -1)
    return live, token_slot[:, None], slot_token[:, None]


BOTH = ("dp", "section")


def hop(value, source, target):
    return lax.ppermute(value, BOTH, [(d * 4 + source, d * 4 + target) for d in range(32)])


def swap(value, sections, from_low=True, from_high=True):
    pairs = []
    for d in range(32):
        if from_low if d < 16 else from_high:
            pairs += [(d * 4 + s, (d + 16) % 32 * 4 + s) for s in sections]
    return lax.ppermute(value, BOTH, pairs)


def local(
    canvas_in,
    conditioning,
    grid_shape,
    kept_rank,
    first_weight,
    second_weight,
    modulation_weight,
    modulation_bias,
    out_grad,
):
    section = lax.axis_index("section")
    low = lax.axis_index("dp") // 16
    low_ref = jnp.reshape(low, (1,)).astype(jnp.int32)
    w1, w2 = first_weight[0], second_weight[0]
    live, token_slot, slot_token = jax.vmap(canvas_layout)(grid_shape)
    scalars = [jnp.stack([live[c], low]).astype(jnp.int32) for c in range(2)]
    kept_scalars = jnp.stack([jnp.int32(KEPT), low]).astype(jnp.int32)
    kept_col = [kept_rank[c][:, None] for c in range(2)]
    kept_row = [kept_rank[c][None, :] for c in range(2)]

    packed_in, packed_grad = move_rows(token_slot, canvas_in, out_grad)
    arrived = [[hop(packed_in[c], s, 0) for s in (1, 2, 3)] for c in range(2)]
    rows0 = [jnp.concatenate([packed_in[c]] + arrived[c], axis=1) for c in range(2)]
    whole_grad = lax.all_gather(packed_grad, "section", axis=2, tiled=True)

    signal = jax.nn.silu(conditioning.astype(F32)).astype(BF)
    modulation = jnp.dot(signal, modulation_weight[0], preferred_element_type=F32) + modulation_bias[0]
    mod = [modulation[c].reshape(3, D) for c in range(2)]
    kept_grad = move_rows(kept_rank[:, :, None], whole_grad)[0]

    low_shape, big_shape, kept_shape = array(VALID, D), array(VALID, FF), array(KEPT, D)
    pair_shape, mod_shape = array(2, VALID, D), array(3, D, dtype=F32)

    def by_section(**branches):
        first = next(iter(branches.values()))
        shapes = jax.eval_shape(first)
        idle = lambda: tuple(unwritten(*shapes))
        return lax.switch(section, [branches.get("s%d" % s, idle) for s in range(4)])

    def attend(c, rows):
        def run():
            out, hidden, joined, branch = attention_forward(VALID, scalars[c], rows, mod[c], w1)
            return (out, hidden, joined, branch) + tuple(unwritten(big_shape, kept_shape))

        return run

    def attend_kept(c, rows):
        def run():
            out, hidden, joined, branch = attention_forward(KEPT, kept_scalars, rows, mod[c], w1)
            return (out, hidden, joined, branch) + tuple(unwritten(big_shape, kept_shape))

        return run

    def feed(c, rows):
        def run():
            out, hidden, active, slope, branch, picked = feed_forward(rows, mod[c], w1, w2, kept_col[c])
            return out, hidden, active, branch, slope, picked

        return run

    t0 = by_section(s0=attend(0, rows0[0]))
    rows1 = [hop(t0[0], 0, 1)]
    t1 = by_section(s0=attend(1, rows0[1]), s1=feed(0, rows1[0]))
    rows1.append(hop(t1[0], 0, 1))
    picked = [hop(t1[5], 1, 2)]
    t2 = by_section(s1=feed(1, rows1[1]), s2=attend_kept(0, picked[0]))
    picked.append(hop(t2[5], 1, 2))
    rows3 = [hop(t2[0][:KEPT], 2, 3)]

    def both(c, rows):
        def run():
            out, hidden, active, grad, bg, ig, modgrad = feed_both(rows, mod[c], w1, w2, kept_grad[c])
            return (out, grad) + tuple(unwritten(pair_shape)) + (bg, modgrad, hidden, active, low_shape_of(), ig)

        return run

    def low_shape_of():
        return unwritten(low_shape)[0]

    def attend_three(c, rows):
        def run():
            out, hidden, joined, branch = attention_forward(KEPT, kept_scalars, rows, mod[c], w1)
            grad, kept, bg, modgrad, ig = unwritten(low_shape, pair_shape, low_shape, mod_shape, big_shape)
            return out, grad, kept, bg, modgrad, hidden, joined, branch, ig

        return run

    t3 = by_section(s2=attend_three(1, picked[1]), s3=both(0, rows3[0]))
    rows3.append(hop(t3[0][:KEPT], 2, 3))
    back2 = [hop(t3[1][:KEPT], 3, 2)]
    done = [hop(t3[0][:KEPT], 3, 1)]

    def back_kept(c, rows, joined, branch, up):
        def run():
            grad, kept, sent, modgrad = attention_backward(KEPT, kept_scalars, rows, mod[c], w1, joined, branch, up)
            return grad, kept, sent, modgrad

        return run

    def both_four(c, rows):
        def run():
            out, hidden, active, grad, bg, ig, modgrad = feed_both(rows, mod[c], w1, w2, kept_grad[c])
            kept, sent = unwritten(pair_shape, pair_shape)
            return grad, kept, sent, modgrad, out, hidden, active, bg, ig

        return run

    def back_kept_four(*a):
        run = back_kept(*a)
        return lambda: run() + tuple(unwritten(low_shape, low_shape, big_shape, low_shape, big_shape))

    t4 = by_section(s2=back_kept_four(0, picked[0], t2[2], t2[3], back2[0]), s3=both_four(1, rows3[1]))
    back2.append(hop(t4[0][:KEPT], 3, 2))
    done.append(hop(t4[4][:KEPT], 3, 1))
    back1 = [hop(t4[0][:KEPT], 2, 1)]

    def back_feed(c, rows, slope, branch, kept):
        def run():
            grad, bg, ig, modgrad = feed_backward(
                rows, mod[c], w1, w2, slope, branch, whole_grad[c], kept, kept_row[c]
            )
            return (grad,) + tuple(unwritten(pair_shape, pair_shape)) + (modgrad, bg, ig)

        return run

    def back_whole(c, rows, joined, branch, up):
        def run():
            return tuple(attention_backward(VALID, scalars[c], rows, mod[c], w1, joined, branch, up))

        return run

    def padded(run):
        return lambda: tuple(run()) + tuple(unwritten(low_shape, big_shape))

    t5 = by_section(
        s1=back_feed(0, rows1[0], t1[4], t1[3], back1[0]),
        s2=padded(back_kept(1, picked[1], t3[6], t3[7], back2[1])),
    )
    back1.append(hop(t5[0][:KEPT], 2, 1))
    back0 = [hop(t5[0], 1, 0)]
    t6 = by_section(
        s1=back_feed(1, rows1[1], t2[4], t2[3], back1[1]),
        s0=padded(back_whole(0, rows0[0], t0[2], t0[3], back0[0])),
    )
    back0.append(hop(t6[0], 1, 0))
    t7 = by_section(s0=back_whole(1, rows0[1], t1[2], t1[3], back0[1]))

    hid = [swap(t0[1], (0,)), swap(t1[1], (0, 1)), swap(t2[1], (1, 2)), swap(t3[5], (2, 3)), swap(t4[5], (3,))]
    mixed = [
        swap(t0[2][:, 3 * D :], (0,), from_high=False),
        swap(t1[2][:, 3 * D :], (0,), from_high=False),
        swap(t2[2][:, 3 * D :], (2,), from_high=False),
        swap(t3[6][:, 3 * D :], (2,), from_high=False),
    ]
    bg3, bg4 = swap(t3[3], (3,)), swap(t4[7], (3,))
    sent4, sent5 = swap(t4[2], (2,)), swap(t5[2], (2,))
    bg5, bg6 = swap(t5[4], (1,)), swap(t6[4], (1,))
    sent6, sent7 = swap(t6[2], (0,)), swap(t7[2], (0,))

    def weights_attention():
        first = attention_weights(
            VALID, low_ref, (t6[1], t7[1], sent6, sent7), (t0[1], t1[1], hid[0], hid[1]), (t0[2], t1[2]), mixed[:2]
        )
        return (first,) + tuple(unwritten(array(HALF, D)))

    def weights_attention_kept():
        first = attention_weights(
            KEPT, low_ref, (t4[1], t5[1], sent4, sent5), (t2[1], t3[5], hid[2], hid[3]), (t2[2], t3[6]), mixed[2:]
        )
        return (first,) + tuple(unwritten(array(HALF, D)))

    def weights_feed():
        return tuple(
            feed_weights(
                VALID, low_ref, (t1[1], t2[1]), (hid[1], hid[2]), (t5[4], t6[4]), (bg5, bg6),
                (t1[2], t2[2]), (t5[5], t6[5]), w1, w2,
            )
        )

    def weights_feed_kept():
        return tuple(
            feed_weights(
                KEPT, low_ref, (t3[5], t4[5]), (hid[3], hid[4]), (t3[3], t4[7]), (bg3, bg4),
                (t3[6], t4[6]), (t3[8], t4[8]), w1, w2,
            )
        )

    first_part, second_part = by_section(
        s0=weights_attention, s1=weights_feed, s2=weights_attention_kept, s3=weights_feed_kept
    )
    first_sum, second_sum = sum_blocks(first_part, second_part)

    rows4 = [merge((t1, t2)[c][0], done[c], kept_row[c]) for c in range(2)]

    def spread(rows, source):
        parts = [jnp.stack([rows[c][:, q * QUARTER : (q + 1) * QUARTER] for c in range(2)]) for q in range(4)]
        total = None
        for q in range(4):
            if q == source:
                here = jnp.where(section == q, parts[q], jnp.zeros_like(parts[q]))
            else:
                here = hop(parts[q], source, q)
            total = here if total is None else jnp.where(section == q, here, total)
        return total

    result = move_rows(slot_token, spread(rows4, 1))[0]
    canvas_grad = move_rows(slot_token, spread([t6[0], t7[0]], 0))[0]

    def chosen(*values):
        return lax.select_n(section, *values)

    modgrads = jnp.stack(
        [chosen(t6[3], t5[3], t4[3], t3[4]).reshape(-1), chosen(t7[3], t6[3], t5[3], t4[3]).reshape(-1)]
    )
    all_modgrads = lax.all_gather(modgrads.astype(BF), "dp", axis=0, tiled=True)
    all_signal = lax.all_gather(signal, "dp", axis=0, tiled=True)
    modulation_grad = mm(all_signal, all_modgrads, TN)
    bias_grad = jnp.sum(all_modgrads.astype(F32), axis=0)
    return (
        result,
        canvas_grad,
        first_sum.T[None],
        second_sum[None],
        modulation_grad[None],
        bias_grad[None],
    )


def solution(mesh):
    placed = (
        P("dp", None, "section"),
        P("dp", None),
        P("dp"),
        P("dp", None),
        P("section", None, None),
        P("section", None, None),
        P("section", None, None),
        P("section", None),
        P("dp", None, "section"),
    )
    return jax.shard_map(
        local,
        mesh=mesh,
        in_specs=placed,
        out_specs=(
            P("dp", None, "section"),
            P("dp", None, "section"),
            P("section", None, "dp"),
            P("section", "dp", None),
            P("section", None, None),
            P("section", None),
        ),
        check_vma=False,
    )
```

time: 1710 us -> 559 us (0.33)
  waiting for transfers between devices: 667 us -> 46.4 us
  other arithmetic: 305 us -> 17 us
  local copies, waits for them, and re-layouts: 257 us -> 40.6 us
  Pallas kernels: 0 us -> 108 us
  loops' own time: 135 us -> 27.1 us
  matrix products: 91.2 us -> 12.5 us
  starting transfers between devices: 71.4 us -> 101 us
  blocking collectives: 161 us -> 182 us
    reduce_scatter x2 -> x0, waiting for transfers between devices: 360 us -> none  [the longest x1 183 us: local(): lax.psum_scatter(first_total.astype(jnp.bfloat16), 'dp', scatter_dimensio...]
    psum x2 -> x0, waiting for transfers between devices: 264 us -> none  [the longest x1 264 us: local(): lax.psum(local_product.astype(jnp.bfloat16), 'dp').astype(jnp.float32)]
    add x10 -> x0, other arithmetic: 183 us -> none  [the longest x5 108 us: backward_tick(): first_total = first_total + first_part]
    all_gather x0 -> x2, blocking collectives: none -> 182 us  [the longest x1 95 us: local(): all_modgrads = lax.all_gather(modgrads.astype(BF), 'dp', axis=0, tiled=True)]
    psum x1 -> x0, blocking collectives: 161 us -> none  [local(): lax.psum(jnp.sum(modulation_grads, axis=0).astype(jnp.bfloat16), 'dp')]
    pallas_call x0 -> x19, Pallas kernels: none -> 108 us  [the longest x2 37.4 us: attention_backward(): pl.pallas_call(attention_backward_kernel, grid=(4,), in_specs=[pl.BlockSp...]
    another operation x12 -> x9, loops' own time: 135 us -> 27.1 us  [by_section(): lax.switch(section, [branches.get('s%d' % s, idle) for s in range(4)])]
    dot_general x34 -> x2, matrix products: 91.2 us -> 12.5 us  [the longest x1 8.14 us: mm(): return lax.dot_general(a, b, dims, preferred_element_type=F32)]
  transfers between devices with their start and end apart: 16 -> 44, of which waited for: 10 -> 8; matrix products, arithmetic and copies ran while one was open for 17% -> 10% of each run, Pallas kernels for 0% -> 12%
where the time goes in v1:
time: 559 us; the launch traced here: 551 us
  blocking collectives  182 us (33%)
  Pallas kernels  108 us (19%)
  starting transfers between devices  101 us (18%)
  waiting for transfers between devices  46.4 us (8%)
  local copies, waits for them, and re-layouts  40.6 us (7%)
  loops' own time  27.1 us (5%)
  other arithmetic  17 us (3%)
  between operations  15.5 us (3%)
  matrix products  12.5 us (2%)
    all_gather x1, blocking collectives, local(): all_modgrads = lax.all_gather(modgrads.astype(BF), 'dp', axis=0, tiled=True)  95 us
    all_gather x1, blocking collectives, local(): all_signal = lax.all_gather(signal, 'dp', axis=0, tiled=True)  87.3 us
    ppermute x26, starting transfers between devices, hop(): lax.ppermute(value, BOTH, [(d * 4 + source, d * 4 + target) for d in rang...  70.9 us
    ppermute x26, waiting for transfers between devices, hop(): lax.ppermute(value, BOTH, [(d * 4 + source, d * 4 + target) for d in rang...  38.3 us
    pallas_call x2, Pallas kernels, attention_backward(): pl.pallas_call(attention_backward_kernel, grid=(4,), in_specs=[pl.BlockSp...  37.4 us
    pallas_call x1, Pallas kernels, sum_blocks(): pl.pallas_call(sum_kernel, in_specs=[spec] * 2, out_specs=[spec] * 2, out...  31.5 us
    ppermute x17, starting transfers between devices, swap(): return lax.ppermute(value, BOTH, pairs)  30.3 us
    another operation x9, loops' own time, by_section(): lax.switch(section, [branches.get('s%d' % s, idle) for s in range(4)])  27.1 us
  transfers between devices with their start and end apart: 44, of which 8 were waited for; matrix products, arithmetic and copies ran while one was open for 10% of the time, Pallas kernels for 12%

profile of v1, /device:TPU:2, one launch (start us, length us, event | category | flops | bytes accessed | tf_op | source)
XLA Modules:
  0.0 550.8 jit_solution(13330516063742709347)
XLA Ops:
  12.0 5.0 fusion.13.refs_0_
  22.8 4.4 fusion.2
  31.6 11.9 %conditional.9 = ((bf16[256,1152]{1,0:T(8,128)(2,1)S(1)}, bf16[256,1152]{1,0:T(8,128)(2,1)}, bf16[256,4608]{1,0:T(8,128)(2,1)}, bf16[256,1152]{1,0:T(8,128)(2,1)})) conditional(s32[]{:T(128)} %clamp.2, (s32[2]{0:T(128)}, bf16[256,1152]{1,0:T(8,128)(2,1)}, f32[3,1152]{1,0:T(4,128)S(1)}, ...), branch_computations={%region_0.1_spmd, %region_1.2_spmd, %region_2.3_spmd, %region_3.4_... | conditional | flops 2717908992 | bytes 10616840 | solution.py:785
  31.8 11.4 %attention_forward.4 = (bf16[256,1152]{1,0:T(8,128)(2,1)S(1)}, bf16[256,1152]{1,0:T(8,128)(2,1)}, bf16[256,4608]{1,0:T(8,128)(2,1)}, bf16[256,1152]{1,0:T(8,128)(2,1)}) custom-call(s32[2]{0:T(128)} %get-tuple-element.312.live_ref, bf16[256,1152]{1,0:T(8,128)(2,1)} %get-tuple-element.313.rows_ref, f32[3,1152]{1,0:T(4,128)S(1)} %get-tuple-element.314.mod_ref, ...), custom_call_target="tpu_custom_call" | custom-call | flops 2717908992 | bytes 10616832 | tf_op jit(solution)/shard_map/cond/branch_0_fun/attention_forward/pallas_call | solution.py:156
  49.9 6.6 %collective-permute-done.1 = bf16[256,288]{1,0:T(8,128)(2,1)S(1)} collective-permute-done((bf16[256,288]{1,0:T(8,128)(2,1)S(1)}, bf16[256,288]{1,0:T(8,128)(2,1)S(1)}, u32[]{:S(2)}, u32[]{:S(2)}) %collective-permute-start.1) | collective-permute-done | bytes 147488 | tf_op jit(solution)/shard_map/ppermute | solution.py:736
  58.5 11.2 %conditional.10 = ((bf16[256,1152]{1,0:T(8,128)(2,1)S(1)}, bf16[256,1152]{1,0:T(8,128)(2,1)}, bf16[256,4608]{1,0:T(8,128)(2,1)}, bf16[256,1152]{1,0:T(8,128)(2,1...) conditional(s32[]{:T(128)} %clamp.2, (s32[2]{0:T(128)}, ...), branch_computations={%region_4.5_spmd, %region_5.6_spmd, %region_6.7_spmd, %region_7.8_... | conditional | flops 5435817984 | bytes 21234744 | solution.py:785
  58.5 11.2 %attention_forward.5 = (bf16[256,1152]{1,0:T(8,128)(2,1)S(1)}, bf16[256,1152]{1,0:T(8,128)(2,1)}, bf16[256,4608]{1,0:T(8,128)(2,1)}, bf16[256,1152]{1,0:T(8,128)(2,1)}) custom-call(s32[2]{0:T(128)} %get-tuple-element.328.live_ref, bf16[256,1152]{1,0:T(8,128)(2,1)} %get-tuple-element.329.rows_ref, f32[3,1152]{1,0:T(4,128)S(1)} %get-tuple-element.330.mod_ref, ...), custom_call_target="tpu_custom_call" | custom-call | flops 2717908992 | bytes 10616832 | tf_op jit(solution)/shard_map/cond/branch_0_fun/attention_forward/pallas_call | solution.py:156
  69.7 2.2 collective-permute-start.7
  73.4 5.6 %conditional.11 = ((bf16[256,1152]{1,0:T(8,128)(2,1)S(1)}, bf16[256,1152]{1,0:T(8,128)(2,1)}, bf16[256,4608]{1,0:T(8,128)(2,1)}, bf16[256,1152]{1,0:T(8,128)(2,1...) conditional(s32[]{:T(128)} %clamp.2, () %tuple.166, ...), branch_computations={%region_8.9_spmd, %region_9.10_spmd, %region_10.11_spmd, %region_1... | conditional | flops 5435817984 | bytes 21234744 | solution.py:785
  81.3 3.4 copy.34.refs_1_
  85.9 1.7 slice.138
  92.1 8.3 %conditional.13 = (bf16[2,256,1152]{2,1,0:T(8,128)(2,1)}, bf16[2,256,1152]{2,1,0:T(8,128)(2,1)}, f32[3,1152]{1,0:T(4,128)}, bf16[256,1152]{1,0:T(8,128)(2,1)}, b...) conditional(s32[]{:T(128)} %clamp.2, () %tuple.172, () %tuple.173, ...), branch_computations={%region_16.17_spmd, %region_17.18_spmd, %region_18.19_spmd, %regio... | conditional | flops 5435817984 | bytes 21823560 | solution.py:785
  103.4 1.7 slice.141
  109.8 1.7 slice.150
  122.0 87.3 %all-gather = bf16[32,2,1152]{2,1,0:T(2,128)(2,1)} all-gather(bf16[1,2,1152]{2,1,0:T(2,128)(2,1)S(1)} %fusion.31), channel_id=1, replica_groups=mesh['dp'=32,'section'=4] {'dp'}, dimensions={0}, use_global_device_ids=true | all-gather | bytes 152064 | tf_op jit(solution)/shard_map/all_gather | solution.py:963
  209.3 1.6 reshape.436
  211.0 1.5 collective-permute-start.37
  212.5 1.5 collective-permute-start.41
  214.0 28.4 %conditional.15 = ((bf16[256,1152]{1,0:T(8,128)(2,1)}, bf16[2,256,1152]{2,1,0:T(8,128)(2,1)}, bf16[2,256,1152]{2,1,0:T(8,128)(2,1)}, f32[3,1152]{1,0:T(4,128)}, ...) conditional(s32[]{:T(128)} %clamp.2, (s32[2]{0:T(128)}, ...), branch_computations={%region_24.25_spmd, %region_25.26_spmd, %region_26.27_spmd, %regio... | conditional | flops 5435817984 | bytes 24774740 | solution.py:785
  214.2 18.9 %attention_backward.6 = (bf16[256,1152]{1,0:T(8,128)(2,1)}, bf16[2,256,1152]{2,1,0:T(8,128)(2,1)}, bf16[2,256,1152]{2,1,0:T(8,128)(2,1)}, f32[3,1152]{1,0:T(4,128)}) custom-call(s32[2]{0:T(128)} %get-tuple-element.486.live_ref, bf16[256,1152]{1,0:T(8,128)(2,1)} %get-tuple-element.487.rows_ref, f32[3,1152]{1,0:T(4,128)} %get-tuple-element.488.mod_ref, ...), custom_call_target="tpu_custom_call" | custom-call | flops 2717908992 | bytes 10616832 | tf_op jit(solution)/shard_map/cond/branch_0_fun/attention_backward/pallas_call | solution.py:245
  242.4 1.5 collective-permute-start.40
  243.9 1.5 collective-permute-start.42
  246.9 2.0 slice.159
  248.9 1.9 slice.160
  250.8 2.0 slice.161
  256.3 3.5 collective-permute-start.29
  262.8 1.7 collective-permute-start.35
  264.5 29.7 %collective-permute-done.22 = bf16[256,1152]{1,0:T(8,128)(2,1)} collective-permute-done((bf16[256,1152]{1,0:T(8,128)(2,1)}, bf16[256,1152]{1,0:T(8,128)(2,1)}, u32[]{:S(2)}, u32[]{:S(2)}) %collective-permute-start.22) | collective-permute-done | bytes 589856 | tf_op jit(solution)/shard_map/ppermute | solution.py:736
  294.1 1.7 collective-permute-start.36
  295.8 2.3 slice_bitcast_fusion.13
  298.1 18.8 %conditional.16 = (bf16[256,1152]{1,0:T(8,128)(2,1)S(1)}, bf16[2,256,1152]{2,1,0:T(8,128)(2,1)}, bf16[2,256,1152]{2,1,0:T(8,128)(2,1)}, bf16[3,1152]{1,0:T(4,128)(2,1)S(1)}) conditional(s32[]{:T(128)} %clamp.2, (s32[2]{0:T(128)}, bf16[256,1152]{1,0:T(8,128)(2,1)}, f32[3,1152]{1,0:T(4,128)S(1)}, ...), branch_computations={%region_28.29_spmd, %region_29.30_spmd, %region_30.31_spmd, %regio... | conditional | flops 2717912576 | bytes 10637600 | solution.py:785
  298.2 18.5 %attention_backward.7 = (bf16[256,1152]{1,0:T(8,128)(2,1)S(1)}, bf16[2,256,1152]{2,1,0:T(8,128)(2,1)}, bf16[2,256,1152]{2,1,0:T(8,128)(2,1)}, f32[3,1152]{1,0:T(4,128)S(1)}) custom-call(s32[2]{0:T(128)} %get-tuple-element.514.live_ref, bf16[256,1152]{1,0:T(8,128)(2,1)} %get-tuple-element.515.rows_ref, f32[3,1152]{1,0:T(4,128)S(1)} %get-tuple-element.516.mod_ref, ...), custom_call_target="tpu_custom_call" | custom-call | flops 2717908992 | bytes 10616832 | tf_op jit(solution)/shard_map/cond/branch_0_fun/attention_backward/pallas_call | solution.py:245
  319.6 1.8 pad_maximum_fusion.3
  323.1 3.8 collective-permute-start.26
  326.9 2.1 collective-permute-start.23
  329.0 39.1 %collective-permute-start.24 = (bf16[2,256,288]{2,1,0:T(8,128)(2,1)}, bf16[2,256,288]{2,1,0:T(8,128)(2,1)}, u32[]{:S(2)}, u32[]{:S(2)}) collective-permute-start(bf16[2,256,288]{2,1,0:T(8,128)(2,1)} %pad_maximum_fusion.4), channel_id=1, source_target_pairs={{0,2},{4,6},{8,10},{12,14},{16,18},{20,22},{24,26},{28,30},{32,34}... | collective-permute-start | bytes 884744 | tf_op jit(solution)/shard_map/ppermute | solution.py:736
  368.1 2.1 collective-permute-start.25
  370.2 2.2 collective-permute-start.27
  372.4 95.0 %all-gather.1 = bf16[32,2,3456]{2,1,0:T(2,128)(2,1)} all-gather(bf16[1,2,3456]{2,1,0:T(2,128)(2,1)S(1)} %maximum_bitcast_fusion), channel_id=1, replica_groups=mesh['dp'=32,'section'=4] {'dp'}, dimensions={0}, use_global_device_ids=true | all-gather | bytes 456192 | tf_op jit(solution)/shard_map/all_gather | solution.py:962
  468.6 3.7 collective-permute-start.28
  475.6 8.1 %convolution_bitcast_fusion = f32[1,1152,3456]{2,1,0:T(8,128)} fusion(bf16[64,1152]{1,0:T(8,128)(2,1)S(1)} %copy-done.17, bf16[64,3456]{1,0:T(8,128)(2,1)S(1)} %reshape.438), kind=kOutput, calls=%fused_computation.4 | convolution fusion | flops 509607936 | bytes 16515072 | tf_op jit(solution)/shard_map/dot_general | solution.py:36
  485.4 1.6 collective-permute-done.30
  487.0 6.3 %collective-permute-done.31 = bf16[256,1152]{1,0:T(8,128)(2,1)} collective-permute-done((bf16[256,1152]{1,0:T(8,128)(2,1)}, bf16[256,1152]{1,0:T(8,128)(2,1)}, u32[]{:S(2)}, u32[]{:S(2)}) %collective-permute-start.31) | collective-permute-done | bytes 589856 | tf_op jit(solution)/shard_map/ppermute | solution.py:744
  493.3 14.7 %conditional.17 = (bf16[4,4,144,1152]{3,2,1,0:T(8,128)(2,1)}, bf16[4,4,144,1152]{3,2,1,0:T(8,128)(2,1)}) conditional(s32[]{:T(128)} %clamp.2, (s32[1]{0:T(128)}, bf16[2,256,1152]{2,1,0:T(8,128)(2,1)}, bf16[2,256,1152]{2,1,0:T(8,128)(2,1)}, bf16[2,256,1152]{2,1,0:T(8,128)(2,1)}, bf16[2,256,1152]{2,1,0:T(8,128)(2,1)}, ...), branch_computations={%region_32.33_spmd, %region_33.34_spmd, %region_34.35_spmd, %regio... | conditional | flops 16307453952 | bytes 21233680 | solution.py:785
  493.3 11.7 %attention_weights.2 = bf16[2304,1152]{1,0:T(8,128)(2,1)} custom-call(s32[1]{0:T(128)} %get-tuple-element.521.low_ref, bf16[2,256,1152]{2,1,0:T(8,128)(2,1)} %get-tuple-element.522.refs_0_, bf16[2,256,1152]{2,1,0:T(8,128)(2,1)} %get-tuple-element.523.refs_1_, bf16[2,256,1152]{2,1,0:T(8,128)(2,1)} %get-tuple-element.524.refs_2_, ...), custom_call_target="tpu_custom_call" | custom-call | flops 5435817984 | bytes 5308416 | tf_op jit(solution)/shard_map/cond/branch_0_fun/attention_weights/pallas_call | solution.py:288
  508.0 31.5 %sum_blocks.1 = (f32[144,1152]{1,0:T(8,128)}, f32[144,1152]{1,0:T(8,128)}) custom-call(bf16[4,4,144,1152]{3,2,1,0:T(8,128)(2,1)} %get-tuple-element.688.first_ref, bf16[4,4,144,1152]{3,2,1,0:T(8,128)(2,1)} %get-tuple-element.689.second_ref), custom_call_target="tpu_custom_call" | custom-call | flops 5308416 | bytes 21233664 | tf_op jit(solution)/shard_map/sum_blocks/pallas_call | solution.py:702
  539.5 2.0 copy.247
  541.5 2.0 copy.248
  (198 shorter events, 68.9 us)
Async XLA Ops:
  7.2 74.1 %all-gather.4.cloned.1.call-start = ((), (), s32[]{:S(2)}) async-start(), calls=%async_computation | async-start | bytes 1474560 | tf_op jit(solution)/shard_map/all_gather | solution.py:771
  17.9 11.3 %collective-permute-start.3 = (bf16[256,288]{1,0:T(8,128)(2,1)S(1)}, bf16[256,288]{1,0:T(8,128)(2,1)S(1)}, u32[]{:S(2)}, u32[]{:S(2)}) collective-permute-start(bf16[256,288]{1,0:T(8,128)(2,1)S(1)} %get-tuple-element.769), channel_id=1, source_target_pairs={{1,0},{5,4},{9,8},{13,12},{17,16},{21,20},{25,24},{29,28},{33,32},... | collective-permute-start | bytes 442376 | tf_op jit(solution)/shard_map/ppermute | solution.py:736
  19.2 10.5 %collective-permute-start.4 = (bf16[256,288]{1,0:T(8,128)(2,1)S(1)}, bf16[256,288]{1,0:T(8,128)(2,1)S(1)}, u32[]{:S(2)}, u32[]{:S(2)}) collective-permute-start(bf16[256,288]{1,0:T(8,128)(2,1)S(1)} %get-tuple-element.769), channel_id=1, source_target_pairs={{2,0},{6,4},{10,8},{14,12},{18,16},{22,20},{26,24},{30,28},{34,32}... | collective-permute-start | bytes 442376 | tf_op jit(solution)/shard_map/ppermute | solution.py:736
  20.5 9.9 %collective-permute-start.5 = (bf16[256,288]{1,0:T(8,128)(2,1)S(1)}, bf16[256,288]{1,0:T(8,128)(2,1)S(1)}, u32[]{:S(2)}, u32[]{:S(2)}) collective-permute-start(bf16[256,288]{1,0:T(8,128)(2,1)S(1)} %get-tuple-element.769), channel_id=1, source_target_pairs={{3,0},{7,4},{11,8},{15,12},{19,16},{23,20},{27,24},{31,28},{35,32}... | collective-permute-start | bytes 442376 | tf_op jit(solution)/shard_map/ppermute | solution.py:736
  43.5 15.0 %collective-permute-start.6 = (bf16[256,1152]{1,0:T(8,128)(2,1)S(1)}, bf16[256,1152]{1,0:T(8,128)(2,1)S(1)}, u32[]{:S(2)}, u32[]{:S(2)}) collective-permute-start(bf16[256,1152]{1,0:T(8,128)(2,1)S(1)} %get-tuple-element.643), channel_id=1, source_target_pairs={{0,1},{4,5},{8,9},{12,13},{16,17},{20,21},{24,25},{28,29},{32,33},... | collective-permute-start | bytes 1769480 | tf_op jit(solution)/shard_map/ppermute | solution.py:736
  44.8 5.1 collective-permute-start
  46.1 10.5 %collective-permute-start.1 = (bf16[256,288]{1,0:T(8,128)(2,1)S(1)}, bf16[256,288]{1,0:T(8,128)(2,1)S(1)}, u32[]{:S(2)}, u32[]{:S(2)}) collective-permute-start(bf16[256,288]{1,0:T(8,128)(2,1)S(1)} %get-tuple-element.770), channel_id=1, source_target_pairs={{2,0},{6,4},{10,8},{14,12},{18,16},{22,20},{26,24},{30,28},{34,32}... | collective-permute-start | bytes 442376 | tf_op jit(solution)/shard_map/ppermute | solution.py:736
  47.4 9.9 %collective-permute-start.2 = (bf16[256,288]{1,0:T(8,128)(2,1)S(1)}, bf16[256,288]{1,0:T(8,128)(2,1)S(1)}, u32[]{:S(2)}, u32[]{:S(2)}) collective-permute-start(bf16[256,288]{1,0:T(8,128)(2,1)S(1)} %get-tuple-element.770), channel_id=1, source_target_pairs={{3,0},{7,4},{11,8},{15,12},{19,16},{23,20},{27,24},{31,28},{35,32}... | collective-permute-start | bytes 442376 | tf_op jit(solution)/shard_map/ppermute | solution.py:736
  48.7 62.8 %copy-start.27 = (s32[1,128]{1,0:T(1,128)}, s32[1,128]{1,0:T(1,128)S(1)}, u32[]{:S(2)}) copy-start(s32[1,128]{1,0:T(1,128)S(1)} %get-tuple-element.774.index_ref) | copy-start | bytes 1540
  69.7 3.0 collective-permute-start.7
  71.9 0.8 collective-permute-start.8
  79.0 1.6 collective-permute-start.9
  79.7 5.4 collective-permute-start.10
  87.6 4.4 collective-permute-start.13
  90.0 2.1 collective-permute-start.12
  91.4 14.5 %collective-permute-start.11 = (bf16[128,1152]{1,0:T(8,128)(2,1)}, bf16[128,1152]{1,0:T(8,128)(2,1)S(1)}, u32[]{:S(2)}, u32[]{:S(2)}) collective-permute-start(bf16[128,1152]{1,0:T(8,128)(2,1)} %slice.138), channel_id=1, source_target_pairs={{3,1},{7,5},{11,9},{15,13},{19,17},{23,21},{27,25},{31,29},{35,33}... | collective-permute-start | bytes 884744 | tf_op jit(solution)/shard_map/ppermute | solution.py:736
  101.4 7.0 %collective-permute-start.18 = (bf16[128,1152]{1,0:T(8,128)(2,1)S(1)}, bf16[128,1152]{1,0:T(8,128)(2,1)}, u32[]{:S(2)}, u32[]{:S(2)}) collective-permute-start(bf16[128,1152]{1,0:T(8,128)(2,1)S(1)} %slice.149), channel_id=1, source_target_pairs={{2,1},{6,5},{10,9},{14,13},{18,17},{22,21},{26,25},{30,29},{34,33}... | collective-permute-start | bytes 884744 | tf_op jit(solution)/shard_map/ppermute | solution.py:736
  102.8 5.6 %collective-permute-start.19 = (bf16[128,1152]{1,0:T(8,128)(2,1)S(1)}, bf16[128,1152]{1,0:T(8,128)(2,1)S(1)}, u32[]{:S(2)}, u32[]{:S(2)}) collective-permute-start(bf16[128,1152]{1,0:T(8,128)(2,1)S(1)} %slice.149), channel_id=1, source_target_pairs={{3,2},{7,6},{11,10},{15,14},{19,18},{23,22},{27,26},{31,30},{35,34... | collective-permute-start | bytes 884744 | tf_op jit(solution)/shard_map/ppermute | solution.py:736
  105.1 6.4 %collective-permute-start.14 = (bf16[128,1152]{1,0:T(8,128)(2,1)}, bf16[128,1152]{1,0:T(8,128)(2,1)S(1)}, u32[]{:S(2)}, u32[]{:S(2)}) collective-permute-start(bf16[128,1152]{1,0:T(8,128)(2,1)} %slice.141), channel_id=1, source_target_pairs={{3,1},{7,5},{11,9},{15,13},{19,17},{23,21},{27,25},{31,29},{35,33}... | collective-permute-start | bytes 884744 | tf_op jit(solution)/shard_map/ppermute | solution.py:736
  108.4 104.1 %collective-permute-start.20 = (bf16[256,1152]{1,0:T(8,128)(2,1)}, bf16[256,1152]{1,0:T(8,128)(2,1)}, u32[]{:S(2)}, u32[]{:S(2)}) collective-permute-start(bf16[256,1152]{1,0:T(8,128)(2,1)} %get-tuple-element.661), channel_id=1, source_target_pairs={{1,0},{5,4},{9,8},{13,12},{17,16},{21,20},{25,24},{29,28},{33,32},... | collective-permute-start | bytes 1769480 | tf_op jit(solution)/shard_map/ppermute | solution.py:736
  113.0 101.0 %copy-start = (bf16[2,256,1152]{1,0,2:T(2,128)(2,1)S(1)}, bf16[2,256,1152]{1,0,2:T(2,128)(2,1)}, u32[]{:S(2)}) copy-start(bf16[2,256,1152]{1,0,2:T(2,128)(2,1)} %all-gather.4.cloned.1.call-done) | copy-start | bytes 3538948
  114.8 127.6 %collective-permute-start.15 = (bf16[2,256,288]{2,1,0:T(8,128)(2,1)}, bf16[2,256,288]{2,1,0:T(8,128)(2,1)}, u32[]{:S(2)}, u32[]{:S(2)}) collective-permute-start(bf16[2,256,288]{2,1,0:T(8,128)(2,1)} %pad_maximum_fusion), channel_id=1, source_target_pairs={{1,3},{5,7},{9,11},{13,15},{17,19},{21,23},{25,27},{29,31},{33,35}... | collective-permute-start | bytes 884744 | tf_op jit(solution)/shard_map/ppermute | solution.py:736
  117.0 126.9 %collective-permute-start.16 = (bf16[2,256,288]{2,1,0:T(8,128)(2,1)}, bf16[2,256,288]{2,1,0:T(8,128)(2,1)}, u32[]{:S(2)}, u32[]{:S(2)}) collective-permute-start(bf16[2,256,288]{2,1,0:T(8,128)(2,1)} %pad_maximum_fusion.1), channel_id=1, source_target_pairs={{1,2},{5,6},{9,10},{13,14},{17,18},{21,22},{25,26},{29,30},{33,34}... | collective-permute-start | bytes 884744 | tf_op jit(solution)/shard_map/ppermute | solution.py:736
  119.3 126.1 %collective-permute-start.17 = (bf16[2,256,288]{2,1,0:T(8,128)(2,1)}, bf16[2,256,288]{2,1,0:T(8,128)(2,1)}, u32[]{:S(2)}, u32[]{:S(2)}) collective-permute-start(bf16[2,256,288]{2,1,0:T(8,128)(2,1)} %pad_maximum_fusion.2), channel_id=1, source_target_pairs={{1,0},{5,4},{9,8},{13,12},{17,16},{21,20},{25,24},{29,28},{33,32},... | collective-permute-start | bytes 884744 | tf_op jit(solution)/shard_map/ppermute | solution.py:736
  120.6 90.4 %collective-permute-start.21 = (bf16[128,1152]{1,0:T(8,128)(2,1)}, bf16[128,1152]{1,0:T(8,128)(2,1)}, u32[]{:S(2)}, u32[]{:S(2)}) collective-permute-start(bf16[128,1152]{1,0:T(8,128)(2,1)} %slice.150), channel_id=1, source_target_pairs={{2,1},{6,5},{10,9},{14,13},{18,17},{22,21},{26,25},{30,29},{34,33}... | collective-permute-start | bytes 884744 | tf_op jit(solution)/shard_map/ppermute | solution.py:736
  211.0 45.3 %collective-permute-start.37 = (bf16[256,1152]{1,0:T(8,128)(2,1)}, bf16[256,1152]{1,0:T(8,128)(2,1)}, u32[]{:S(2)}, u32[]{:S(2)}) collective-permute-start(bf16[256,1152]{1,0:T(8,128)(2,1)} %get-tuple-element.681), channel_id=1, source_target_pairs={{2,66},{3,67},{6,70},{7,71},{10,74},{11,75},{14,78},{15,79},{18,82... | collective-permute-start | bytes 1769480 | tf_op jit(solution)/shard_map/ppermute | solution.py:744
  212.5 47.3 %collective-permute-start.41 = (bf16[256,1152]{1,0:T(8,128)(2,1)}, bf16[256,1152]{1,0:T(8,128)(2,1)}, u32[]{:S(2)}, u32[]{:S(2)}) collective-permute-start(bf16[256,1152]{1,0:T(8,128)(2,1)} %get-tuple-element.683), channel_id=1, source_target_pairs={{3,67},{7,71},{11,75},{15,79},{19,83},{23,87},{27,91},{31,95},{35,... | collective-permute-start | bytes 1769480 | tf_op jit(solution)/shard_map/ppermute | solution.py:744
  242.4 18.9 %collective-permute-start.40 = (bf16[256,1152]{1,0:T(8,128)(2,1)}, bf16[256,1152]{1,0:T(8,128)(2,1)}, u32[]{:S(2)}, u32[]{:S(2)}) collective-permute-start(bf16[256,1152]{1,0:T(8,128)(2,1)} %get-tuple-element.682), channel_id=1, source_target_pairs={{3,67},{7,71},{11,75},{15,79},{19,83},{23,87},{27,91},{31,95},{35,... | collective-permute-start | bytes 1769480 | tf_op jit(solution)/shard_map/ppermute | solution.py:744
  243.9 18.9 %collective-permute-start.42 = (bf16[256,1152]{1,0:T(8,128)(2,1)}, bf16[256,1152]{1,0:T(8,128)(2,1)}, u32[]{:S(2)}, u32[]{:S(2)}) collective-permute-start(bf16[256,1152]{1,0:T(8,128)(2,1)} %get-tuple-element.684), channel_id=1, source_target_pairs={{3,67},{7,71},{11,75},{15,79},{19,83},{23,87},{27,91},{31,95},{35,... | collective-permute-start | bytes 1769480 | tf_op jit(solution)/shard_map/ppermute | solution.py:744
  245.4 48.7 %collective-permute-start.22 = (bf16[256,1152]{1,0:T(8,128)(2,1)}, bf16[256,1152]{1,0:T(8,128)(2,1)}, u32[]{:S(2)}, u32[]{:S(2)}) collective-permute-start(bf16[256,1152]{1,0:T(8,128)(2,1)} %get-tuple-element.663), channel_id=1, source_target_pairs={{1,0},{5,4},{9,8},{13,12},{17,16},{21,20},{25,24},{29,28},{33,32},... | collective-permute-start | bytes 1769480 | tf_op jit(solution)/shard_map/ppermute | solution.py:736
  256.3 60.7 %collective-permute-start.29 = (bf16[256,1152]{1,0:T(8,128)(2,1)}, bf16[256,1152]{1,0:T(8,128)(2,1)}, u32[]{:S(2)}, u32[]{:S(2)}) collective-permute-start(bf16[256,1152]{1,0:T(8,128)(2,1)} %get-tuple-element.671), channel_id=1, source_target_pairs={{0,64},{1,65},{4,68},{5,69},{8,72},{9,73},{12,76},{13,77},{16,80},... | collective-permute-start | bytes 1769480 | tf_op jit(solution)/shard_map/ppermute | solution.py:744
  259.8 58.1 %collective-permute-start.32 = (bf16[256,1152]{1,0:T(8,128)(2,1)}, bf16[256,1152]{1,0:T(8,128)(2,1)}, u32[]{:S(2)}, u32[]{:S(2)}) collective-permute-start(bf16[256,1152]{1,0:T(8,128)(2,1)} %get-tuple-element.672), channel_id=1, source_target_pairs={{1,65},{2,66},{5,69},{6,70},{9,73},{10,74},{13,77},{14,78},{17,81}... | collective-permute-start | bytes 1769480 | tf_op jit(solution)/shard_map/ppermute | solution.py:744
  261.3 57.4 %collective-permute-start.38 = (bf16[256,1152]{1,0:T(8,128)(2,1)}, bf16[256,1152]{1,0:T(8,128)(2,1)}, u32[]{:S(2)}, u32[]{:S(2)}) collective-permute-start(bf16[256,1152]{1,0:T(8,128)(2,1)} %slice.161), channel_id=1, source_target_pairs={{2,66},{6,70},{10,74},{14,78},{18,82},{22,86},{26,90},{30,94},{34,... | collective-permute-start | bytes 1769480 | tf_op jit(solution)/shard_map/ppermute | solution.py:744
  262.8 66.2 %collective-permute-start.35 = (bf16[2,256,1152]{2,1,0:T(8,128)(2,1)}, bf16[2,256,1152]{2,1,0:T(8,128)(2,1)}, u32[]{:S(2)}, u32[]{:S(2)}) collective-permute-start(bf16[2,256,1152]{2,1,0:T(8,128)(2,1)} %get-tuple-element.679), channel_id=1, source_target_pairs={{2,66},{6,70},{10,74},{14,78},{18,82},{22,86},{26,90},{30,94},{34,... | collective-permute-start | bytes 3538952 | tf_op jit(solution)/shard_map/ppermute | solution.py:744
  294.1 76.1 %collective-permute-start.36 = (bf16[2,256,1152]{2,1,0:T(8,128)(2,1)}, bf16[2,256,1152]{2,1,0:T(8,128)(2,1)}, u32[]{:S(2)}, u32[]{:S(2)}) collective-permute-start(bf16[2,256,1152]{2,1,0:T(8,128)(2,1)} %get-tuple-element.680), channel_id=1, source_target_pairs={{2,66},{6,70},{10,74},{14,78},{18,82},{22,86},{26,90},{30,94},{34,... | collective-permute-start | bytes 3538952 | tf_op jit(solution)/shard_map/ppermute | solution.py:744
  317.1 6.0 %collective-permute-start.39 = (bf16[256,1152]{1,0:T(8,128)(2,1)}, bf16[256,1152]{1,0:T(8,128)(2,1)S(1)}, u32[]{:S(2)}, u32[]{:S(2)}) collective-permute-start(bf16[256,1152]{1,0:T(8,128)(2,1)} %slice.162), channel_id=1, source_target_pairs={{2,66},{6,70},{10,74},{14,78},{18,82},{22,86},{26,90},{30,94},{34,... | collective-permute-start | bytes 1769480 | tf_op jit(solution)/shard_map/ppermute | solution.py:744
  317.9 9.0 %collective-permute-start.33 = (bf16[256,1152]{1,0:T(8,128)(2,1)}, bf16[256,1152]{1,0:T(8,128)(2,1)S(1)}, u32[]{:S(2)}, u32[]{:S(2)}) collective-permute-start(bf16[256,1152]{1,0:T(8,128)(2,1)} %get-tuple-element.673), channel_id=1, source_target_pairs={{1,65},{5,69},{9,73},{13,77},{17,81},{21,85},{25,89},{29,93},{33,9... | collective-permute-start | bytes 1769480 | tf_op jit(solution)/shard_map/ppermute | solution.py:744
  318.6 49.5 %collective-permute-start.34 = (bf16[256,1152]{1,0:T(8,128)(2,1)}, bf16[256,1152]{1,0:T(8,128)(2,1)S(1)}, u32[]{:S(2)}, u32[]{:S(2)}) collective-permute-start(bf16[256,1152]{1,0:T(8,128)(2,1)} %get-tuple-element.674), channel_id=1, source_target_pairs={{1,65},{5,69},{9,73},{13,77},{17,81},{21,85},{25,89},{29,93},{33,9... | collective-permute-start | bytes 1769480 | tf_op jit(solution)/shard_map/ppermute | solution.py:744
  319.6 156.0 %copy-start.17 = (bf16[64,1152]{1,0:T(8,128)(2,1)S(1)}, bf16[64,1152]{1,0:T(8,128)(2,1)}, u32[]{:S(2)}) copy-start(bf16[64,1152]{1,0:T(8,128)(2,1)} %reshape.436) | copy-start | bytes 442372
  323.1 49.3 %copy-start.19 = (bf16[256,1152]{1,0:T(8,128)(2,1)}, bf16[256,1152]{1,0:T(8,128)(2,1)S(1)}, u32[]{:S(2)}) copy-start(bf16[256,1152]{1,0:T(8,128)(2,1)S(1)} %collective-permute-done.39) | copy-start | bytes 1769476
  323.1 170.3 %collective-permute-start.26 = (bf16[2,256,1152]{2,1,0:T(8,128)(2,1)}, bf16[2,256,1152]{2,1,0:T(8,128)(2,1)}, u32[]{:S(2)}, u32[]{:S(2)}) collective-permute-start(bf16[2,256,1152]{2,1,0:T(8,128)(2,1)} %get-tuple-element.668), channel_id=1, source_target_pairs={{0,64},{4,68},{8,72},{12,76},{16,80},{20,84},{24,88},{28,92},{32,9... | collective-permute-start | bytes 3538952 | tf_op jit(solution)/shard_map/ppermute | solution.py:744
  326.9 141.7 %collective-permute-start.23 = (bf16[2,256,288]{2,1,0:T(8,128)(2,1)}, bf16[2,256,288]{2,1,0:T(8,128)(2,1)}, u32[]{:S(2)}, u32[]{:S(2)}) collective-permute-start(bf16[2,256,288]{2,1,0:T(8,128)(2,1)} %pad_maximum_fusion.3), channel_id=1, source_target_pairs={{0,3},{4,7},{8,11},{12,15},{16,19},{20,23},{24,27},{28,31},{32,35}... | collective-permute-start | bytes 884744 | tf_op jit(solution)/shard_map/ppermute | solution.py:736
  329.0 143.3 %collective-permute-start.24 = (bf16[2,256,288]{2,1,0:T(8,128)(2,1)}, bf16[2,256,288]{2,1,0:T(8,128)(2,1)}, u32[]{:S(2)}, u32[]{:S(2)}) collective-permute-start(bf16[2,256,288]{2,1,0:T(8,128)(2,1)} %pad_maximum_fusion.4), channel_id=1, source_target_pairs={{0,2},{4,6},{8,10},{12,14},{16,18},{20,22},{24,26},{28,30},{32,34}... | collective-permute-start | bytes 884744 | tf_op jit(solution)/shard_map/ppermute | solution.py:736
  368.1 105.5 %collective-permute-start.25 = (bf16[2,256,288]{2,1,0:T(8,128)(2,1)}, bf16[2,256,288]{2,1,0:T(8,128)(2,1)}, u32[]{:S(2)}, u32[]{:S(2)}) collective-permute-start(bf16[2,256,288]{2,1,0:T(8,128)(2,1)} %pad_maximum_fusion.5), channel_id=1, source_target_pairs={{0,1},{4,5},{8,9},{12,13},{16,17},{20,21},{24,25},{28,29},{32,33},... | collective-permute-start | bytes 884744 | tf_op jit(solution)/shard_map/ppermute | solution.py:736
  370.2 123.2 %collective-permute-start.27 = (bf16[2,256,1152]{2,1,0:T(8,128)(2,1)}, bf16[2,256,1152]{2,1,0:T(8,128)(2,1)}, u32[]{:S(2)}, u32[]{:S(2)}) collective-permute-start(bf16[2,256,1152]{2,1,0:T(8,128)(2,1)} %get-tuple-element.669), channel_id=1, source_target_pairs={{0,64},{4,68},{8,72},{12,76},{16,80},{20,84},{24,88},{28,92},{32,9... | collective-permute-start | bytes 3538952 | tf_op jit(solution)/shard_map/ppermute | solution.py:744
  468.6 16.8 %collective-permute-start.28 = (bf16[256,1152]{1,0:T(8,128)(2,1)}, bf16[256,1152]{1,0:T(8,128)(2,1)}, u32[]{:S(2)}, u32[]{:S(2)}) collective-permute-start(bf16[256,1152]{1,0:T(8,128)(2,1)} %get-tuple-element.670), channel_id=1, source_target_pairs={{0,64},{4,68},{8,72},{12,76},{16,80},{20,84},{24,88},{28,92},{32,9... | collective-permute-start | bytes 1769480 | tf_op jit(solution)/shard_map/ppermute | solution.py:744
  472.3 14.7 %collective-permute-start.30 = (bf16[256,1152]{1,0:T(8,128)(2,1)}, bf16[256,1152]{1,0:T(8,128)(2,1)}, u32[]{:S(2)}, u32[]{:S(2)}) collective-permute-start(bf16[256,1152]{1,0:T(8,128)(2,1)} %slice.159), channel_id=1, source_target_pairs={{0,64},{4,68},{8,72},{12,76},{16,80},{20,84},{24,88},{28,92},{32,9... | collective-permute-start | bytes 1769480 | tf_op jit(solution)/shard_map/ppermute | solution.py:744
  473.6 19.7 %collective-permute-start.31 = (bf16[256,1152]{1,0:T(8,128)(2,1)}, bf16[256,1152]{1,0:T(8,128)(2,1)}, u32[]{:S(2)}, u32[]{:S(2)}) collective-permute-start(bf16[256,1152]{1,0:T(8,128)(2,1)} %slice.160), channel_id=1, source_target_pairs={{0,64},{4,68},{8,72},{12,76},{16,80},{20,84},{24,88},{28,92},{32,9... | collective-permute-start | bytes 1769480 | tf_op jit(solution)/shard_map/ppermute | solution.py:744
  (29 other events, 414.2 us)
Sparse Core Ops, SparseCore 0:
  22.9 24.4 all-gather.3
